TPU v7x, 256 devices: a whole 4x4x8 slice. The times are simulated.
256 devices in a mesh: along: 16 (over y, x), cross: 8 (over z), depth: 2 (over core).
Axes of the slice: x: 4, y: 4, z: 8, core: 2. Of those that a mesh axis runs over, the one named last changes fastest.
Arguments:
- offsets: float32 [3, 64, 32, 4, 128], P(None, 'along', 'cross', 'depth'), may hold values from 0 to 1
- velocity: float32 [3, 64, 32, 4, 128], P(None, 'along', 'cross', 'depth'), may hold values from -3 to 3
- density: float32 [64, 32, 4, 128], P('along', 'cross', 'depth'), may hold values from 0.97 to 1.03
- mass: float32 [64, 32, 4, 128], P('along', 'cross', 'depth'), may hold values from 0.004 to 0.012
- pairs: int32 [26, 64, 32, 4], P(None, 'along', 'cross', 'depth'), may hold values from 0 to 1, as said below
Outputs:
- rates: float32 [4, 64, 32, 4, 128], P(None, 'along', 'cross', 'depth')
- advanced: float32 [7, 64, 32, 4, 128], P(None, 'along', 'cross', 'depth')
Inputs may be any that keep to these rules, and one draw needn't show every extreme that they name: A flag marks a tile that may hold pairs within reach: the particles of each block lie in a box inside its cell, and the flag is 1 exactly when the boxes of the two blocks, placed at their grid positions, are less than 1 apart. The flags are symmetric: pairs[k] at block b equals pairs[25 - k] at the block b + (offset k); a flag whose neighbour block lies outside the grid of 64 x 32 x 4 blocks is 0.
All inputs are finite; a program needn't handle non-finite values.
Results may differ from a plain program's by a relative error of at most 0.0001.
Values sent between devices are 32-bit elements; how exact they have to be, the bound alone decides.
A program may use at most 64 MiB of HBM per device.

v0:
```python
import math

import jax
import jax.numpy as jnp
import numpy as np
from jax import lax
from jax.sharding import PartitionSpec as P

SMOOTH = 0.5
SOUND_SPEED = 10.0
ARTIFICIAL = 0.5
TIME_STEP = 0.01
STIFFNESS = SOUND_SPEED * SOUND_SPEED / 7.0
KERNEL = 105.0 / (16.0 * math.pi * SMOOTH**5)
GRAVITY = (0.0, 0.35, 0.0, -0.94)
tile_group = 32


def with_halo(cells, sides, width):
    for axis, dim in sides:
        count = lax.axis_size(axis)
        ends = count - 1
        head = lax.slice_in_dim(cells, 0, width, axis=dim)
        tail = lax.slice_in_dim(cells, cells.shape[dim] - width, cells.shape[dim], axis=dim)
        cells = jnp.concatenate(
            [
                lax.ppermute(tail, axis, [(i, (i + 1) % count) for i in range(ends)]),
                cells,
                lax.ppermute(head, axis, [((i + 1) % count, i) for i in range(ends)]),
            ],
            axis=dim,
        )
    return cells


def pressure_term(dens_value):
    return STIFFNESS * (dens_value**7 - 1.0) / (dens_value * dens_value)


def pair_terms(left_block, right_block, shift_vec):
    separation = [
        left_block[..., component, :, None]
        - right_block[..., component, None, :]
        - shift_vec[..., component, None, None]
        for component in range(3)
    ]
    relative = [
        left_block[..., 3 + component, :, None] - right_block[..., 3 + component, None, :]
        for component in range(3)
    ]
    dist_sq = (
        separation[0] * separation[0]
        + separation[1] * separation[1]
        + separation[2] * separation[2]
    )
    support = jnp.maximum(1.0 - jnp.sqrt(dist_sq), 0.0)
    kernel_grad = -KERNEL * support * support * support
    closing = (
        relative[0] * separation[0] + relative[1] * separation[1] + relative[2] * separation[2]
    )
    approach = SMOOTH * closing / (dist_sq + 0.01 * SMOOTH * SMOOTH)
    dens_left = left_block[..., 6, :, None]
    dens_right = right_block[..., 6, None, :]
    visc_term = (
        -ARTIFICIAL * SOUND_SPEED * jnp.minimum(approach, 0.0) * 2.0 / (dens_left + dens_right)
    )
    scalar_term = (pressure_term(dens_left) + pressure_term(dens_right) + visc_term) * kernel_grad
    flux_term = closing * kernel_grad
    mass_left = left_block[..., 7, :, None]
    mass_right = right_block[..., 7, None, :]
    near_force = scalar_term * mass_right
    far_force = scalar_term * mass_left
    left_rates = jnp.stack(
        [jnp.sum(flux_term * mass_right, -1)]
        + [-jnp.sum(near_force * sep, -1) for sep in separation],
        -2,
    )
    right_rates = jnp.stack(
        [jnp.sum(flux_term * mass_left, -2)] + [jnp.sum(far_force * sep, -2) for sep in separation],
        -2,
    )
    return (left_rates, right_rates)


def owned_offsets():
    chosen_ids = []
    for offset_id in range(27):
        steps = (offset_id // 9 - 1, offset_id // 3 % 3 - 1, offset_id % 3 - 1)
        total = steps[0] + steps[1] + steps[2]
        leading = [value for value in steps if value != 0]
        if offset_id == 13 or total > 0 or (total == 0 and leading[0] > 0):
            chosen_ids.append(offset_id)
    return chosen_ids


def tile_tables(span_a, span_c, span_d, offset_ids):
    pad_c = span_c + 2
    pad_d = span_d + 2
    lefts, rights, shifts, listed_ids, sides, owners = ([], [], [], [], [], [])
    owner_id = 0
    for along_pos in range(span_a):
        for cross_pos in range(span_c):
            for depth_pos in range(span_d):
                own_pad = ((along_pos + 1) * pad_c + cross_pos + 1) * pad_d + depth_pos + 1
                for offset_id in offset_ids:
                    step_a = offset_id // 9 - 1
                    step_c = offset_id // 3 % 3 - 1
                    step_d = offset_id % 3 - 1
                    lefts.append(own_pad)
                    rights.append(
                        ((along_pos + 1 + step_a) * pad_c + cross_pos + 1 + step_c) * pad_d
                        + depth_pos
                        + 1
                        + step_d
                    )
                    shifts.append([step_a, step_c, step_d])
                    if offset_id == 13:
                        listed_ids.append(-1)
                        sides.append(0)
                    else:
                        listed_ids.append(offset_id if offset_id < 13 else offset_id - 1)
                        sides.append(1)
                    owners.append(owner_id)
                owner_id += 1
    return (
        np.array(lefts),
        np.array(rights),
        np.array(shifts, dtype=np.float32),
        np.array(listed_ids),
        np.array(sides, dtype=np.float32),
        np.array(owners),
    )


def send_back(grid):
    rim_pair = jnp.stack([grid[:, 0], grid[:, -1]], axis=1)
    arrived = with_halo(rim_pair, (("along", 1),), 1)
    interior = grid[:, 1:-1]
    interior = interior.at[:, 0].add(arrived[:, 0])
    interior = interior.at[:, -1].add(arrived[:, 3])
    rim_pair = jnp.stack([interior[:, :, 0], interior[:, :, -1]], axis=2)
    arrived = with_halo(rim_pair, (("cross", 2),), 1)
    interior = interior[:, :, 1:-1]
    interior = interior.at[:, :, 0].add(arrived[:, :, 0])
    interior = interior.at[:, :, -1].add(arrived[:, :, 3])
    rim_pair = jnp.stack([interior[:, :, :, 0], interior[:, :, :, -1]], axis=3)
    arrived = with_halo(rim_pair, (("depth", 3),), 1)
    interior = interior[:, :, :, 1:-1]
    interior = interior.at[:, :, :, 0].add(arrived[:, :, :, 0])
    interior = interior.at[:, :, :, -1].add(arrived[:, :, :, 3])
    return interior


def evaluate_local(packed, pairs):
    span_a, span_c, span_d, block_width = (
        packed.shape[1],
        packed.shape[2],
        packed.shape[3],
        packed.shape[4],
    )
    padded = with_halo(packed, (("along", 1), ("cross", 2), ("depth", 3)), 1)
    pad_a, pad_c, pad_d = (span_a + 2, span_c + 2, span_d + 2)
    flat_blocks = jnp.moveaxis(padded, 0, 3).reshape(pad_a * pad_c * pad_d, 8, block_width)
    offset_ids = owned_offsets()
    left_np, right_np, shift_np, listed_np, side_np, owner_np = tile_tables(
        span_a, span_c, span_d, offset_ids
    )
    real_count = left_np.shape[0]
    padding_count = -real_count % tile_group
    left_table = jnp.asarray(
        np.concatenate([left_np, np.full(padding_count, left_np[0])]), jnp.int32
    )
    right_table = jnp.asarray(
        np.concatenate([right_np, np.full(padding_count, left_np[0])]), jnp.int32
    )
    shift_table = jnp.asarray(
        np.concatenate([shift_np, np.zeros((padding_count, 3), np.float32)]), jnp.float32
    )
    side_table = jnp.asarray(
        np.concatenate([side_np, np.zeros(padding_count, np.float32)]), jnp.float32
    )
    listed = pairs.reshape(26, span_a * span_c * span_d)
    active_real = jnp.where(
        jnp.asarray(listed_np >= 0), listed[np.maximum(listed_np, 0), owner_np], 1
    )
    active = jnp.concatenate([active_real, jnp.zeros((padding_count,), jnp.int32)])
    tile_order = jnp.argsort(1 - active, stable=True)
    live_count = jnp.sum(active)
    turn_count = (live_count + tile_group - 1) // tile_group
    right_live = jnp.where(active > 0, right_table, left_table)

    def one_turn(turn_id, accumulated):
        chosen = lax.dynamic_slice_in_dim(tile_order, turn_id * tile_group, tile_group)
        left_ids = left_table[chosen]
        right_ids = right_live[chosen]
        weight = active[chosen].astype(jnp.float32)[:, None, None]
        left_rates, right_rates = pair_terms(
            flat_blocks[left_ids], flat_blocks[right_ids], shift_table[chosen]
        )
        accumulated = accumulated.at[left_ids].add(weight * left_rates)
        accumulated = accumulated.at[right_ids].add(
            weight * side_table[chosen][:, None, None] * right_rates
        )
        return accumulated

    accumulated = jnp.zeros((pad_a * pad_c * pad_d, 4, block_width), jnp.float32)
    accumulated = lax.fori_loop(0, turn_count, one_turn, accumulated)
    grid = jnp.moveaxis(accumulated.reshape(pad_a, pad_c, pad_d, 4, block_width), 3, 0)
    interior = send_back(grid)
    return interior + jnp.array(GRAVITY, jnp.float32).reshape(4, 1, 1, 1, 1)


def shards(offsets, velocity, density, mass, pairs):
    half_step = 0.5 * TIME_STEP
    packed = jnp.concatenate([offsets, velocity, density[None], mass[None]], 0)
    first_rates = evaluate_local(packed, pairs)
    moved_offsets = offsets + half_step * velocity
    velocity_half = velocity + half_step * first_rates[1:]
    density_half = density + half_step * first_rates[0]
    packed_half = jnp.concatenate([moved_offsets, velocity_half, density_half[None], mass[None]], 0)
    second_rates = evaluate_local(packed_half, pairs)
    velocity_corr = velocity + half_step * second_rates[1:]
    density_corr = density + half_step * second_rates[0]
    offsets_corr = offsets + half_step * velocity_corr
    advanced = jnp.concatenate(
        [
            2.0 * offsets_corr - offsets,
            2.0 * velocity_corr - velocity,
            (2.0 * density_corr - density)[None],
        ],
        0,
    )
    return (second_rates, advanced)


def solution(mesh):
    return jax.shard_map(
        shards,
        mesh=mesh,
        in_specs=(
            P(None, "along", "cross", "depth", None),
            P(None, "along", "cross", "depth", None),
            P("along", "cross", "depth", None),
            P("along", "cross", "depth", None),
            P(None, "along", "cross", "depth"),
        ),
        out_specs=(
            P(None, "along", "cross", "depth", None),
            P(None, "along", "cross", "depth", None),
        ),
        check_vma=False,
    )
```

profile of v0, /device:TPU:1, one launch (start us, length us, event | category | flops | bytes accessed | tf_op | source)
XLA Modules:
  0.0 575.9 jit_solution(18425522070292451753)
XLA Ops:
  1.6 3.9 collective-permute-start
  21.5 5.3 collective-permute-start.5
  33.3 179.1 %while.40 = (s32[]{:T(128)}, f32[144,4,128]{2,1,0:T(4,128)S(1)}, s32[]{:T(128)}, s32[448]{0:T(512)S(1)}, s32[448]{0:T(512)S(1)}, /*index=5*/f32[144,8,128]{2,1,0...) while((s32[]{:T(128)}, f32[144,4,128]{2,1,0:T(4,128)S(1)}, ...), condition=%wide.region_15.16_spmd.clone, body=%wide.region_4.15_spmd.sunk.clone.sunk | while | flops 27991428 | bytes 2574519 | solution.py:207
  38.4 9.0 %multiply_reduce_fusion.18 = (f32[32,128]{1,0:T(8,128)S(1)}, f32[32,128]{1,0:T(8,128)S(1)}, f32[32,128]{1,0:T(8,128)S(1)}, f32[32,128]{1,0:T(8,128)S(1)}, f32[32...) fusion(f32[32,128]{1,0:T(8,128)S(1)} %bitcast.278, ...), kind=kLoop, calls=%fused_computation.23.clone.1 | loop fusion | flops 27754496 | bytes 426368 | tf_op jit(solution)/shard_map/while/body/reduce_sum | solution.py:79
  56.3 9.0 %multiply_reduce_fusion.18 = (f32[32,128]{1,0:T(8,128)S(1)}, f32[32,128]{1,0:T(8,128)S(1)}, f32[32,128]{1,0:T(8,128)S(1)}, f32[32,128]{1,0:T(8,128)S(1)}, f32[32...) fusion(f32[32,128]{1,0:T(8,128)S(1)} %bitcast.278, ...), kind=kLoop, calls=%fused_computation.23.clone.1 | loop fusion | flops 27754496 | bytes 426368 | tf_op jit(solution)/shard_map/while/body/reduce_sum | solution.py:79
  74.3 9.0 %multiply_reduce_fusion.18 = (f32[32,128]{1,0:T(8,128)S(1)}, f32[32,128]{1,0:T(8,128)S(1)}, f32[32,128]{1,0:T(8,128)S(1)}, f32[32,128]{1,0:T(8,128)S(1)}, f32[32...) fusion(f32[32,128]{1,0:T(8,128)S(1)} %bitcast.278, ...), kind=kLoop, calls=%fused_computation.23.clone.1 | loop fusion | flops 27754496 | bytes 426368 | tf_op jit(solution)/shard_map/while/body/reduce_sum | solution.py:79
  92.2 9.0 %multiply_reduce_fusion.18 = (f32[32,128]{1,0:T(8,128)S(1)}, f32[32,128]{1,0:T(8,128)S(1)}, f32[32,128]{1,0:T(8,128)S(1)}, f32[32,128]{1,0:T(8,128)S(1)}, f32[32...) fusion(f32[32,128]{1,0:T(8,128)S(1)} %bitcast.278, ...), kind=kLoop, calls=%fused_computation.23.clone.1 | loop fusion | flops 27754496 | bytes 426368 | tf_op jit(solution)/shard_map/while/body/reduce_sum | solution.py:79
  110.1 9.0 %multiply_reduce_fusion.18 = (f32[32,128]{1,0:T(8,128)S(1)}, f32[32,128]{1,0:T(8,128)S(1)}, f32[32,128]{1,0:T(8,128)S(1)}, f32[32,128]{1,0:T(8,128)S(1)}, f32[32...) fusion(f32[32,128]{1,0:T(8,128)S(1)} %bitcast.278, ...), kind=kLoop, calls=%fused_computation.23.clone.1 | loop fusion | flops 27754496 | bytes 426368 | tf_op jit(solution)/shard_map/while/body/reduce_sum | solution.py:79
  128.0 9.0 %multiply_reduce_fusion.18 = (f32[32,128]{1,0:T(8,128)S(1)}, f32[32,128]{1,0:T(8,128)S(1)}, f32[32,128]{1,0:T(8,128)S(1)}, f32[32,128]{1,0:T(8,128)S(1)}, f32[32...) fusion(f32[32,128]{1,0:T(8,128)S(1)} %bitcast.278, ...), kind=kLoop, calls=%fused_computation.23.clone.1 | loop fusion | flops 27754496 | bytes 426368 | tf_op jit(solution)/shard_map/while/body/reduce_sum | solution.py:79
  145.9 9.0 %multiply_reduce_fusion.18 = (f32[32,128]{1,0:T(8,128)S(1)}, f32[32,128]{1,0:T(8,128)S(1)}, f32[32,128]{1,0:T(8,128)S(1)}, f32[32,128]{1,0:T(8,128)S(1)}, f32[32...) fusion(f32[32,128]{1,0:T(8,128)S(1)} %bitcast.278, ...), kind=kLoop, calls=%fused_computation.23.clone.1 | loop fusion | flops 27754496 | bytes 426368 | tf_op jit(solution)/shard_map/while/body/reduce_sum | solution.py:79
  163.8 9.0 %multiply_reduce_fusion.18 = (f32[32,128]{1,0:T(8,128)S(1)}, f32[32,128]{1,0:T(8,128)S(1)}, f32[32,128]{1,0:T(8,128)S(1)}, f32[32,128]{1,0:T(8,128)S(1)}, f32[32...) fusion(f32[32,128]{1,0:T(8,128)S(1)} %bitcast.278, ...), kind=kLoop, calls=%fused_computation.23.clone.1 | loop fusion | flops 27754496 | bytes 426368 | tf_op jit(solution)/shard_map/while/body/reduce_sum | solution.py:79
  181.8 9.0 %multiply_reduce_fusion.18 = (f32[32,128]{1,0:T(8,128)S(1)}, f32[32,128]{1,0:T(8,128)S(1)}, f32[32,128]{1,0:T(8,128)S(1)}, f32[32,128]{1,0:T(8,128)S(1)}, f32[32...) fusion(f32[32,128]{1,0:T(8,128)S(1)} %bitcast.278, ...), kind=kLoop, calls=%fused_computation.23.clone.1 | loop fusion | flops 27754496 | bytes 426368 | tf_op jit(solution)/shard_map/while/body/reduce_sum | solution.py:79
  199.7 9.0 %multiply_reduce_fusion.18 = (f32[32,128]{1,0:T(8,128)S(1)}, f32[32,128]{1,0:T(8,128)S(1)}, f32[32,128]{1,0:T(8,128)S(1)}, f32[32,128]{1,0:T(8,128)S(1)}, f32[32...) fusion(f32[32,128]{1,0:T(8,128)S(1)} %bitcast.278, ...), kind=kLoop, calls=%fused_computation.23.clone.1 | loop fusion | flops 27754496 | bytes 426368 | tf_op jit(solution)/shard_map/while/body/reduce_sum | solution.py:79
  212.4 21.0 %collective-permute-start.6 = (f32[4,1,6,4,128]{4,3,2,1,0:T(4,128)S(1)}, f32[4,1,6,4,128]{4,3,2,1,0:T(4,128)S(1)}, u32[]{:S(2)}, u32[]{:S(2)}) collective-permute-start(f32[4,1,6,4,128]{4,3,2,1,0:T(4,128)S(1)} %get-tuple-element.679), channel_id=1, source_target_pairs={{0,16},{16,32},{32,48},{48,64},{64,80},{80,96},{96,112},{112,128},... | collective-permute-start | bytes 147464 | tf_op jit(solution)/shard_map/ppermute | solution.py:27
  242.7 4.6 collective-permute-done.9
  248.8 39.3 %collective-permute-start.11 = (f32[4,4,4,1,128]{4,3,2,1,0:T(1,128)S(1)}, f32[4,4,4,1,128]{4,3,2,1,0:T(1,128)S(1)}, u32[]{:S(2)}, u32[]{:S(2)}) collective-permute-start(f32[4,4,4,1,128]{4,3,2,1,0:T(1,128)S(1)} %get-tuple-element.694), channel_id=1, source_target_pairs={{1,0},{3,2},{5,4},{7,6},{9,8},{11,10},{13,12},{15,14},{17,16},{19,... | collective-permute-start | bytes 98312 | tf_op jit(solution)/shard_map/ppermute | solution.py:29
  297.9 4.5 collective-permute-start.14
  309.2 4.7 collective-permute-start.17
  315.5 179.3 %while.41 = (s32[]{:T(128)}, f32[144,4,128]{2,1,0:T(4,128)S(1)}, s32[]{:T(128)}, s32[448]{0:T(512)S(1)}, s32[448]{0:T(512)S(1)}, /*index=5*/f32[144,8,128]{2,1,0...) while((s32[]{:T(128)}, f32[144,4,128]{2,1,0:T(4,128)S(1)}, ...), condition=%wide.region_27.28_spmd.clone, body=%wide.region_16.27_spmd.sunk.clone.sunk | while | flops 27991428 | bytes 2574519 | solution.py:207
  320.9 9.0 %multiply_reduce_fusion.19 = (f32[32,128]{1,0:T(8,128)S(1)}, f32[32,128]{1,0:T(8,128)S(1)}, f32[32,128]{1,0:T(8,128)S(1)}, f32[32,128]{1,0:T(8,128)S(1)}, f32[32...) fusion(f32[32,128]{1,0:T(8,128)S(1)} %bitcast.285, ...), kind=kLoop, calls=%fused_computation.69.clone.1 | loop fusion | flops 27754496 | bytes 426368 | tf_op jit(solution)/shard_map/while/body/reduce_sum | solution.py:79
  338.8 9.0 %multiply_reduce_fusion.19 = (f32[32,128]{1,0:T(8,128)S(1)}, f32[32,128]{1,0:T(8,128)S(1)}, f32[32,128]{1,0:T(8,128)S(1)}, f32[32,128]{1,0:T(8,128)S(1)}, f32[32...) fusion(f32[32,128]{1,0:T(8,128)S(1)} %bitcast.285, ...), kind=kLoop, calls=%fused_computation.69.clone.1 | loop fusion | flops 27754496 | bytes 426368 | tf_op jit(solution)/shard_map/while/body/reduce_sum | solution.py:79
  356.7 9.0 %multiply_reduce_fusion.19 = (f32[32,128]{1,0:T(8,128)S(1)}, f32[32,128]{1,0:T(8,128)S(1)}, f32[32,128]{1,0:T(8,128)S(1)}, f32[32,128]{1,0:T(8,128)S(1)}, f32[32...) fusion(f32[32,128]{1,0:T(8,128)S(1)} %bitcast.285, ...), kind=kLoop, calls=%fused_computation.69.clone.1 | loop fusion | flops 27754496 | bytes 426368 | tf_op jit(solution)/shard_map/while/body/reduce_sum | solution.py:79
  374.6 9.0 %multiply_reduce_fusion.19 = (f32[32,128]{1,0:T(8,128)S(1)}, f32[32,128]{1,0:T(8,128)S(1)}, f32[32,128]{1,0:T(8,128)S(1)}, f32[32,128]{1,0:T(8,128)S(1)}, f32[32...) fusion(f32[32,128]{1,0:T(8,128)S(1)} %bitcast.285, ...), kind=kLoop, calls=%fused_computation.69.clone.1 | loop fusion | flops 27754496 | bytes 426368 | tf_op jit(solution)/shard_map/while/body/reduce_sum | solution.py:79
  392.5 9.0 %multiply_reduce_fusion.19 = (f32[32,128]{1,0:T(8,128)S(1)}, f32[32,128]{1,0:T(8,128)S(1)}, f32[32,128]{1,0:T(8,128)S(1)}, f32[32,128]{1,0:T(8,128)S(1)}, f32[32...) fusion(f32[32,128]{1,0:T(8,128)S(1)} %bitcast.285, ...), kind=kLoop, calls=%fused_computation.69.clone.1 | loop fusion | flops 27754496 | bytes 426368 | tf_op jit(solution)/shard_map/while/body/reduce_sum | solution.py:79
  410.5 9.0 %multiply_reduce_fusion.19 = (f32[32,128]{1,0:T(8,128)S(1)}, f32[32,128]{1,0:T(8,128)S(1)}, f32[32,128]{1,0:T(8,128)S(1)}, f32[32,128]{1,0:T(8,128)S(1)}, f32[32...) fusion(f32[32,128]{1,0:T(8,128)S(1)} %bitcast.285, ...), kind=kLoop, calls=%fused_computation.69.clone.1 | loop fusion | flops 27754496 | bytes 426368 | tf_op jit(solution)/shard_map/while/body/reduce_sum | solution.py:79
  428.4 9.0 %multiply_reduce_fusion.19 = (f32[32,128]{1,0:T(8,128)S(1)}, f32[32,128]{1,0:T(8,128)S(1)}, f32[32,128]{1,0:T(8,128)S(1)}, f32[32,128]{1,0:T(8,128)S(1)}, f32[32...) fusion(f32[32,128]{1,0:T(8,128)S(1)} %bitcast.285, ...), kind=kLoop, calls=%fused_computation.69.clone.1 | loop fusion | flops 27754496 | bytes 426368 | tf_op jit(solution)/shard_map/while/body/reduce_sum | solution.py:79
  446.3 9.0 %multiply_reduce_fusion.19 = (f32[32,128]{1,0:T(8,128)S(1)}, f32[32,128]{1,0:T(8,128)S(1)}, f32[32,128]{1,0:T(8,128)S(1)}, f32[32,128]{1,0:T(8,128)S(1)}, f32[32...) fusion(f32[32,128]{1,0:T(8,128)S(1)} %bitcast.285, ...), kind=kLoop, calls=%fused_computation.69.clone.1 | loop fusion | flops 27754496 | bytes 426368 | tf_op jit(solution)/shard_map/while/body/reduce_sum | solution.py:79
  464.2 9.0 %multiply_reduce_fusion.19 = (f32[32,128]{1,0:T(8,128)S(1)}, f32[32,128]{1,0:T(8,128)S(1)}, f32[32,128]{1,0:T(8,128)S(1)}, f32[32,128]{1,0:T(8,128)S(1)}, f32[32...) fusion(f32[32,128]{1,0:T(8,128)S(1)} %bitcast.285, ...), kind=kLoop, calls=%fused_computation.69.clone.1 | loop fusion | flops 27754496 | bytes 426368 | tf_op jit(solution)/shard_map/while/body/reduce_sum | solution.py:79
  482.1 9.0 %multiply_reduce_fusion.19 = (f32[32,128]{1,0:T(8,128)S(1)}, f32[32,128]{1,0:T(8,128)S(1)}, f32[32,128]{1,0:T(8,128)S(1)}, f32[32,128]{1,0:T(8,128)S(1)}, f32[32...) fusion(f32[32,128]{1,0:T(8,128)S(1)} %bitcast.285, ...), kind=kLoop, calls=%fused_computation.69.clone.1 | loop fusion | flops 27754496 | bytes 426368 | tf_op jit(solution)/shard_map/while/body/reduce_sum | solution.py:79
  494.9 23.5 %collective-permute-start.18 = (f32[4,1,6,4,128]{4,3,2,1,0:T(4,128)S(1)}, f32[4,1,6,4,128]{4,3,2,1,0:T(4,128)S(1)}, u32[]{:S(2)}, u32[]{:S(2)}) collective-permute-start(f32[4,1,6,4,128]{4,3,2,1,0:T(4,128)S(1)} %get-tuple-element.675), channel_id=1, source_target_pairs={{0,16},{16,32},{32,48},{48,64},{64,80},{80,96},{96,112},{112,128},... | collective-permute-start | bytes 147464 | tf_op jit(solution)/shard_map/ppermute | solution.py:27
  523.3 3.9 collective-permute-start.20
  533.3 40.6 %collective-permute-start.23 = (f32[4,4,4,1,128]{4,3,2,1,0:T(1,128)S(1)}, f32[4,4,4,1,128]{4,3,2,1,0:T(1,128)S(1)}, u32[]{:S(2)}, u32[]{:S(2)}) collective-permute-start(f32[4,4,4,1,128]{4,3,2,1,0:T(1,128)S(1)} %get-tuple-element.690), channel_id=1, source_target_pairs={{1,0},{3,2},{5,4},{7,6},{9,8},{11,10},{13,12},{15,14},{17,16},{19,... | collective-permute-start | bytes 98312 | tf_op jit(solution)/shard_map/ppermute | solution.py:29
  (683 shorter events, 238.8 us)
Async XLA Ops:
  0.6 15.4 %copy-start = (s32[26,4,4,2]{0,3,2,1:T(2,128)S(1)}, s32[26,4,4,2]{0,3,2,1:T(2,128)}, u32[]{:S(2)}) copy-start(s32[26,4,4,2]{0,3,2,1:T(2,128)} %param.57) | copy-start | bytes 9988
  0.6 15.4 %copy-start.3 = (s32[448]{0:T(512)S(1)}, s32[448]{0:T(512)}, u32[]{:S(2)}) copy-start(s32[448]{0:T(512)} %constant.545) | copy-start | bytes 5380
  1.6 5.3 collective-permute-start
  5.6 4.7 collective-permute-start.1
  11.2 8.3 %collective-permute-start.2 = (f32[8,6,1,2,128]{4,3,2,1,0:T(2,128)S(1)}, f32[8,6,1,2,128]{4,3,2,1,0:T(2,128)S(1)}, u32[]{:S(2)}, u32[]{:S(2)}) collective-permute-start(f32[8,6,1,2,128]{4,3,2,1,0:T(2,128)S(1)} %get-tuple-element.688), channel_id=1, source_target_pairs={{0,2},{2,4},{4,6},{6,8},{8,10},{10,12},{12,14},{1,3},{3,5},{5,7},{... | collective-permute-start | bytes 147464 | tf_op jit(solution)/shard_map/ppermute | solution.py:27
  14.8 5.0 collective-permute-start.3
  16.1 3.7 copy-start.5
  16.1 3.7 copy-start.6
  19.5 7.3 %copy-start.1 = (s32[448]{0:T(512)S(1)}, s32[448]{0:T(512)}, u32[]{:S(2)}) copy-start(s32[448]{0:T(512)} %constant.508.clone) | copy-start | bytes 5380
  19.5 7.3 %copy-start.11 = (s32[448]{0:T(512)S(1)}, s32[448]{0:T(512)}, u32[]{:S(2)}) copy-start(s32[448]{0:T(512)} %constant.509.clone) | copy-start | bytes 5380
  19.5 7.3 %copy-start.12 = (pred[448]{0:T(512)(128)(4,1)S(1)}, pred[448]{0:T(512)(128)(4,1)}, u32[]{:S(2)}) copy-start(pred[448]{0:T(512)(128)(4,1)} %constant.512.clone) | copy-start | bytes 1348
  20.2 11.7 %collective-permute-start.4 = (f32[8,6,6,1,128]{4,3,2,1,0:T(1,128)S(1)}, f32[8,6,6,1,128]{4,3,2,1,0:T(1,128)S(1)}, u32[]{:S(2)}, u32[]{:S(2)}) collective-permute-start(f32[8,6,6,1,128]{4,3,2,1,0:T(1,128)S(1)} %get-tuple-element.680), channel_id=1, source_target_pairs={{0,1},{2,3},{4,5},{6,7},{8,9},{10,11},{12,13},{14,15},{16,17},{18,... | collective-permute-start | bytes 442376 | tf_op jit(solution)/shard_map/ppermute | solution.py:27
  21.5 10.4 %collective-permute-start.5 = (f32[8,6,6,1,128]{4,3,2,1,0:T(1,128)S(1)}, f32[8,6,6,1,128]{4,3,2,1,0:T(1,128)S(1)}, u32[]{:S(2)}, u32[]{:S(2)}) collective-permute-start(f32[8,6,6,1,128]{4,3,2,1,0:T(1,128)S(1)} %get-tuple-element.681), channel_id=1, source_target_pairs={{1,0},{3,2},{5,4},{7,6},{9,8},{11,10},{13,12},{15,14},{17,16},{19,... | collective-permute-start | bytes 442376 | tf_op jit(solution)/shard_map/ppermute | solution.py:29
  212.4 22.3 %collective-permute-start.6 = (f32[4,1,6,4,128]{4,3,2,1,0:T(4,128)S(1)}, f32[4,1,6,4,128]{4,3,2,1,0:T(4,128)S(1)}, u32[]{:S(2)}, u32[]{:S(2)}) collective-permute-start(f32[4,1,6,4,128]{4,3,2,1,0:T(4,128)S(1)} %get-tuple-element.679), channel_id=1, source_target_pairs={{0,16},{16,32},{32,48},{48,64},{64,80},{80,96},{96,112},{112,128},... | collective-permute-start | bytes 147464 | tf_op jit(solution)/shard_map/ppermute | solution.py:27
  233.5 4.8 collective-permute-start.7
  238.3 50.8 %copy-start.10 = (f32[4]{0:T(128)S(1)}, f32[4]{0:T(128)}, u32[]{:S(2)}) copy-start(f32[4]{0:T(128)} %constant.516.clone) | copy-start | bytes 52
  238.4 4.3 collective-permute-start.8
  241.4 6.0 %collective-permute-start.9 = (f32[4,4,1,4,128]{4,3,2,1,0:T(4,128)S(1)}, f32[4,4,1,4,128]{4,3,2,1,0:T(4,128)S(1)}, u32[]{:S(2)}, u32[]{:S(2)}) collective-permute-start(f32[4,4,1,4,128]{4,3,2,1,0:T(4,128)S(1)} %get-tuple-element.686), channel_id=1, source_target_pairs={{2,0},{4,2},{6,4},{8,6},{10,8},{12,10},{14,12},{3,1},{5,3},{7,5},{... | collective-permute-start | bytes 98312 | tf_op jit(solution)/shard_map/ppermute | solution.py:29
  247.4 40.7 %collective-permute-start.10 = (f32[4,4,4,1,128]{4,3,2,1,0:T(1,128)S(1)}, f32[4,4,4,1,128]{4,3,2,1,0:T(1,128)S(1)}, u32[]{:S(2)}, u32[]{:S(2)}) collective-permute-start(f32[4,4,4,1,128]{4,3,2,1,0:T(1,128)S(1)} %get-tuple-element.695), channel_id=1, source_target_pairs={{0,1},{2,3},{4,5},{6,7},{8,9},{10,11},{12,13},{14,15},{16,17},{18,... | collective-permute-start | bytes 98312 | tf_op jit(solution)/shard_map/ppermute | solution.py:27
  248.8 40.2 %collective-permute-start.11 = (f32[4,4,4,1,128]{4,3,2,1,0:T(1,128)S(1)}, f32[4,4,4,1,128]{4,3,2,1,0:T(1,128)S(1)}, u32[]{:S(2)}, u32[]{:S(2)}) collective-permute-start(f32[4,4,4,1,128]{4,3,2,1,0:T(1,128)S(1)} %get-tuple-element.694), channel_id=1, source_target_pairs={{1,0},{3,2},{5,4},{7,6},{9,8},{11,10},{13,12},{15,14},{17,16},{19,... | collective-permute-start | bytes 98312 | tf_op jit(solution)/shard_map/ppermute | solution.py:29
  289.5 5.0 collective-permute-start.12
  293.1 4.7 collective-permute-start.13
  297.9 5.8 %collective-permute-start.14 = (f32[8,6,1,2,128]{4,3,2,1,0:T(2,128)S(1)}, f32[8,6,1,2,128]{4,3,2,1,0:T(2,128)S(1)}, u32[]{:S(2)}, u32[]{:S(2)}) collective-permute-start(f32[8,6,1,2,128]{4,3,2,1,0:T(2,128)S(1)} %get-tuple-element.684), channel_id=1, source_target_pairs={{0,2},{2,4},{4,6},{6,8},{8,10},{10,12},{12,14},{1,3},{3,5},{5,7},{... | collective-permute-start | bytes 147464 | tf_op jit(solution)/shard_map/ppermute | solution.py:27
  302.4 5.1 collective-permute-start.15
  307.9 6.0 %collective-permute-start.16 = (f32[8,6,6,1,128]{4,3,2,1,0:T(1,128)S(1)}, f32[8,6,6,1,128]{4,3,2,1,0:T(1,128)S(1)}, u32[]{:S(2)}, u32[]{:S(2)}) collective-permute-start(f32[8,6,6,1,128]{4,3,2,1,0:T(1,128)S(1)} %get-tuple-element.676), channel_id=1, source_target_pairs={{0,1},{2,3},{4,5},{6,7},{8,9},{10,11},{12,13},{14,15},{16,17},{18,... | collective-permute-start | bytes 442376 | tf_op jit(solution)/shard_map/ppermute | solution.py:27
  309.2 5.7 collective-permute-start.17
  494.9 24.8 %collective-permute-start.18 = (f32[4,1,6,4,128]{4,3,2,1,0:T(4,128)S(1)}, f32[4,1,6,4,128]{4,3,2,1,0:T(4,128)S(1)}, u32[]{:S(2)}, u32[]{:S(2)}) collective-permute-start(f32[4,1,6,4,128]{4,3,2,1,0:T(4,128)S(1)} %get-tuple-element.675), channel_id=1, source_target_pairs={{0,16},{16,32},{32,48},{48,64},{64,80},{80,96},{96,112},{112,128},... | collective-permute-start | bytes 147464 | tf_op jit(solution)/shard_map/ppermute | solution.py:27
  518.4 4.8 collective-permute-start.19
  523.3 5.2 collective-permute-start.20
  527.2 4.7 collective-permute-start.21
  532.0 42.0 %collective-permute-start.22 = (f32[4,4,4,1,128]{4,3,2,1,0:T(1,128)S(1)}, f32[4,4,4,1,128]{4,3,2,1,0:T(1,128)S(1)}, u32[]{:S(2)}, u32[]{:S(2)}) collective-permute-start(f32[4,4,4,1,128]{4,3,2,1,0:T(1,128)S(1)} %get-tuple-element.691), channel_id=1, source_target_pairs={{0,1},{2,3},{4,5},{6,7},{8,9},{10,11},{12,13},{14,15},{16,17},{18,... | collective-permute-start | bytes 98312 | tf_op jit(solution)/shard_map/ppermute | solution.py:27
  533.3 41.5 %collective-permute-start.23 = (f32[4,4,4,1,128]{4,3,2,1,0:T(1,128)S(1)}, f32[4,4,4,1,128]{4,3,2,1,0:T(1,128)S(1)}, u32[]{:S(2)}, u32[]{:S(2)}) collective-permute-start(f32[4,4,4,1,128]{4,3,2,1,0:T(1,128)S(1)} %get-tuple-element.690), channel_id=1, source_target_pairs={{1,0},{3,2},{5,4},{7,6},{9,8},{11,10},{13,12},{15,14},{17,16},{19,... | collective-permute-start | bytes 98312 | tf_op jit(solution)/shard_map/ppermute | solution.py:29
  (5 other events, 9.8 us)
where the time goes:
time: 578 us; the launch traced here: 576 us
  other arithmetic  264 us (46%)
  starting transfers between devices  172 us (30%)
  local copies, waits for them, and re-layouts  107 us (19%)
  waiting for transfers between devices  27.9 us (5%)
    reduce_sum x20, other arithmetic, pair_terms(): jnp.sum(flux_term * mass_left, -2)  181 us
    ppermute x12, starting transfers between devices, with_halo(): lax.ppermute(head, axis, [((i + 1) % count, i) for i in range(ends)])  100 us
    ppermute x12, starting transfers between devices, with_halo(): lax.ppermute(tail, axis, [(i, (i + 1) % count) for i in range(ends)])  72.1 us
    scatter-add x20, other arithmetic, one_turn(): accumulated = accumulated.at[left_ids].add(weight * left_rates)  34.4 us
    scatter-add x20, other arithmetic, one_turn(): accumulated.at[right_ids]  33.2 us
    ppermute x12, waiting for transfers between devices, with_halo(): lax.ppermute(head, axis, [((i + 1) % count, i) for i in range(ends)])  27.8 us
    gather x20, local copies, waits for them, and re-layouts, one_turn(): side_table[chosen][:, None, None]  14.3 us
    gather x20, local copies, waits for them, and re-layouts, one_turn(): right_ids = right_live[chosen]  14.3 us
  transfers between devices with their start and end apart: 24, of which 11 were waited for; matrix products, arithmetic and copies ran while one was open for 1% of the time, Pallas kernels for 0%

commit v1 on v0

v1 whole, which is shorter than its diff:
```python
import math

import jax
import jax.numpy as jnp
import numpy as np
from jax import lax
from jax.experimental import pallas as pl
from jax.experimental.pallas import tpu as pltpu
from jax.sharding import PartitionSpec as P

SMOOTH = 0.5
SOUND_SPEED = 10.0
ARTIFICIAL = 0.5
TIME_STEP = 0.01
HALF = 0.5 * TIME_STEP
STIFFNESS = SOUND_SPEED * SOUND_SPEED / 7.0
KERNEL = 105.0 / (16.0 * math.pi * SMOOTH**5)
SOFT = 0.01 * SMOOTH * SMOOTH
VISC = -1.0 / (ARTIFICIAL * SOUND_SPEED * 2.0 * SMOOTH)
MESH = pl.DeviceIdType.MESH
F32 = jnp.float32
BF16 = jnp.bfloat16
W = 128
CHUNK = 32


def shift_table():
    table = np.zeros((9, 80, 2 * W), np.float32)
    for oa in (-1, 0, 1):
        for oc in (-1, 0, 1):
            entry = table[(oa + 1) * 3 + oc + 1]
            for start in (0, 8, 16):
                entry[start : start + 2, :W] = [[2 * oa], [2 * oc]]
                entry[start + 6, :W] = 1
                entry[start + 3 : start + 5, W:] = [[oa], [oc]]
                entry[start + 7, W:] = 1
            for start in (24, 32, 40):
                entry[start : start + 2, :W] = [[-2 * oa], [-2 * oc]]
                entry[start + 3 : start + 5, W:] = [[-oa], [-oc]]
            entry[48, :W] = oa * oa + oc * oc
    return table


def split3(value):
    top = value.astype(BF16).astype(F32)
    rest = value - top
    mid = rest.astype(BF16).astype(F32)
    return top, mid, rest - mid


def derive(raw, layer):
    row = lax.broadcasted_iota(jnp.int32, (8, W), 0)
    lift = (0.0, -1.0, 1.0)[layer]
    state = raw + jnp.where(row == 2, lift, 0.0) if lift else raw
    place = state[0:3]
    speed = state[3:6]
    square = place * place
    mixed = place * speed
    length = square[0:1] + square[1:2] + square[2:3]
    along = mixed[0:1] + mixed[1:2] + mixed[2:3]
    dens = state[6:7]
    mass = state[7:8]
    two = dens * dens
    four = two * two
    press = STIFFNESS * (four * two * dens - 1.0) / two
    plain = jnp.concatenate([place, VISC * dens, press, mass, jnp.zeros((2, W), F32)], 0)
    moments = jnp.concatenate([state[0:6], length, along], 0)
    return moments, plain


def right_tiles(parts):
    row = lax.broadcasted_iota(jnp.int32, (8, W), 0)
    near = []
    mixed = []
    for number, part in enumerate(parts):
        one = 1.0 if number == 0 else 0.0
        near.append(jnp.where(row < 3, -2.0 * part, jnp.where(row == 6, one, 0.0)))
        swapped = jnp.where(row < 3, pltpu.roll(part, 5, 0), pltpu.roll(part, 3, 0))
        mixed.append(jnp.where(row < 6, -swapped, jnp.where(row == 7, one, 0.0)))
    top = jnp.concatenate([jnp.concatenate([near[0], near[1]], 0), jnp.concatenate([mixed[0], mixed[1]], 0)], 1)
    low = jnp.concatenate([jnp.concatenate([near[2], near[0]], 0), jnp.concatenate([mixed[2], mixed[0]], 0)], 1)
    fixed = jnp.concatenate([top.astype(BF16), low.astype(BF16)], 0)
    moved = jnp.concatenate([parts[0], parts[1], parts[2], jnp.ones((8, W), F32)], 0).astype(BF16)
    return fixed, moved


def pair_chunk(dist_sq, closing, col, row, mass_row):
    safe = jnp.maximum(dist_sq, 1e-12)
    reach = jnp.maximum(1.0 - safe * lax.rsqrt(safe), 0.0)
    weight = (reach * reach * reach) * (col[5] * mass_row)
    visc = jnp.minimum(closing, 0.0) / ((safe + SOFT) * (col[3] + row[3]))
    force = weight * (visc + (col[4] + row[4]))
    return [force * (col[0] - row[0]), force * (col[1] - row[1]), force * (col[2] - row[2]), weight * closing]


def fold(values):
    total = values[0:8]
    for start in range(8, values.shape[0], 8):
        total = total + values[start : start + 8]
    return total


def step_kernel(
    counts, off, vel, den, mas, flags, table, rates, adv,
    raw, fixed, moved, plain, lefts, cols, acc_l, acc_r, net, own,
    in_a, in_cp, in_cm, in_d, send_sem, recv_sem,
):
    ai = lax.axis_index("along")
    ci = lax.axis_index("cross")
    di = lax.axis_index("depth")
    n_a, n_c = counts
    prev_a = {"along": lax.rem(ai + n_a - 1, n_a)}
    next_a = {"along": lax.rem(ai + 1, n_a)}
    prev_c = {"cross": lax.rem(ci + n_c - 1, n_c)}
    next_c = {"cross": lax.rem(ci + 1, n_c)}
    other = {"depth": 1 - di}
    sign = (1 - 2 * di).astype(F32)

    barrier = pltpu.get_barrier_semaphore()
    for device in (prev_a, next_a, prev_c, next_c, other):
        pl.semaphore_signal(barrier, inc=1, device_id=device, device_id_type=MESH)
    pl.semaphore_wait(barrier, 5)

    def depth_of(layer):
        return (1 - di) + layer * (2 * di - 1)

    row_id = lax.broadcasted_iota(jnp.int32, (8, W), 0)
    lane_id = lax.broadcasted_iota(jnp.int32, (W, W), 1)
    mirror = jnp.where((row_id == 2) | (row_id == 5), -1.0, 1.0)
    gravity = jnp.where(row_id == 3, 0.35, jnp.where(row_id == 5, -0.94 * sign, 0.0))
    gravity = jnp.where(row_id == 3, 0.35, gravity)
    zero8 = jnp.zeros((8, W), F32)

    def copy(kind, e, src, dst, device):
        return pltpu.make_async_remote_copy(
            src_ref=src, dst_ref=dst, send_sem=send_sem.at[e, kind], recv_sem=recv_sem.at[e, kind],
            device_id=device, device_id_type=MESH,
        )

    def copies(e):
        return (
            copy(0, e, raw.at[e, 0:4, 1:5, 0], raw.at[e, 0:4, 1:5, 2], other),
            copy(1, e, raw.at[e, 0:4, 1], raw.at[e, 0:4, 5], prev_c),
            copy(2, e, raw.at[e, 0, 4], raw.at[e, 0, 0], next_c),
            copy(3, e, raw.at[e, 0], raw.at[e, 4], prev_a),
            copy(4, e, net.at[e, 4], in_a.at[e], next_a),
            copy(5, e, net.at[e, 0:4, 5], in_cp.at[e], next_c),
            copy(6, e, net.at[e, 0, 0], in_cm.at[e], prev_c),
            copy(7, e, net.at[e, 0:4, 1:5, 2], in_d.at[e], other),
        )

    def prepare_right(e, a, c, layer):
        moments, flat = derive(raw[e, a, c, layer], layer)
        parts = split3(moments)
        solid, loose = right_tiles(parts)
        fixed[a, c, layer] = solid
        moved[a, c, layer] = loose
        plain[a, c, layer] = flat
        return parts, flat

    def prepare_own(e, a, c):
        for layer in (0, 1):
            parts, flat = prepare_right(e, a, c + 1, layer)
            d0, d1, d2 = parts
            one = jnp.ones((8, W), F32)
            stack = jnp.concatenate(
                [d0, d0, d1, d1, d0, d2, one, one, one, d0, d1, d2, one, zero8, zero8, flat], 0
            )
            turned = stack.T
            lefts[a * 4 + c, layer * W : layer * W + W] = turned.astype(BF16)
            cols[a * 4 + c, layer * W : layer * W + W] = turned

    def right_side(entry, a, c, layer):
        solid = fixed[a, c, layer]
        loose = moved[a, c, layer]
        bent = jnp.concatenate([loose, loose], 1) * table[entry, 0:32]
        return jnp.concatenate([solid[0:16], solid[0:16], solid[16:32], bent, table[entry, 32:80]], 0)

    def flag_of(base, a, c, layer, right_layer):
        step = (1, 0, 2)[right_layer] - (1, 0, 2)[layer]
        skipped = (1 + (1 - 2 * di) * step) // 2 if isinstance(base, int) else base // 13
        listed = base + 1 + (1 - 2 * di) * step - skipped
        return flags[listed * 32 + (a * 4 + c) * 2 + depth_of(layer)].astype(F32)

    def tiles(p, a, c, qa, qc, entry, base, shift, work, first=False, own_pairs=()):
        left_total = {}
        for right_layer, left_layers, both in work:
            lo, hi = min(left_layers), max(left_layers) + 1
            product = jnp.dot(
                lefts[p, lo * W : hi * W], right_side(entry, qa, qc, right_layer), preferred_element_type=F32
            )
            flat = plain[qa, qc, right_layer]
            placed = flat + shift
            rows = [placed[k : k + 1] for k in range(5)]
            right_total = None
            for layer in left_layers:
                mass_row = flat[5:6]
                if (layer, right_layer) not in own_pairs:
                    mass_row = mass_row * flag_of(base, a, c, layer, right_layer)
                for start in range(0, W, CHUNK):
                    spot = layer * W + start
                    here = product[spot - lo * W : spot - lo * W + CHUNK]
                    col = [cols[p, spot : spot + CHUNK, 120 + k : 121 + k] for k in range(6)]
                    terms = pair_chunk(here[:, :W], here[:, W:], col, rows, mass_row)
                    key = spot
                    if key in left_total:
                        left_total[key] = [x + y for x, y in zip(left_total[key], terms)]
                    else:
                        left_total[key] = terms
                    if layer in both:
                        folded = [fold(x) for x in terms]
                        right_total = folded if right_total is None else [x + y for x, y in zip(right_total, folded)]
            if right_total is not None:
                for k in range(4):
                    acc_r[qa, qc, right_layer, k] += right_total[k]
        for spot, terms in left_total.items():
            for k in range(4):
                if first:
                    acc_l[p, k, spot : spot + CHUNK] = terms[k]
                else:
                    acc_l[p, k, spot : spot + CHUNK] += terms[k]

    def reduced(a, c, layer):
        terms = [jnp.sum(acc_r[a, c, layer, k], 0, keepdims=True) for k in range(4)]
        return jnp.concatenate([jnp.zeros((3, W), F32)] + terms + [jnp.zeros((1, W), F32)], 0)

    def loop(count, body):
        def run(index, carry):
            body(index)
            return carry
        lax.fori_loop(0, count, run, 0)

    def fill(index):
        a, c = index // 4, index % 4
        for layer in (0, 1):
            at = pl.ds(depth_of(layer), 1)
            lines = [off[k, a, c, at, :] - 0.5 for k in range(3)] + [vel[k, a, c, at, :] for k in range(3)]
            lines += [den[a, c, at, :], mas[a, c, at, :]]
            lines[2] = lines[2] * sign
            lines[5] = lines[5] * sign
            raw[0, a, c + 1, layer] = jnp.concatenate(lines, 0)

    loop(16, fill)

    def evaluate(e):
        halo_d, halo_cm, halo_cp, halo_a, back_a, back_cp, back_cm, back_d = copies(e)
        halo_d.start()

        def first_part(index):
            prepare_own(e, index // 4, index % 4)

        loop(16, first_part)

        def clear(index):
            for c in range(6):
                for layer in range(3):
                    for k in range(4):
                        acc_r[index, c, layer, k] = zero8

        loop(5, clear)

        def self_part(index):
            a, c = index // 4, index % 4
            tiles(index, a, c, a, c + 1, 4, 12, 0.0, ((0, (0, 1), (1,)), (1, (1,), ())), True, ((0, 0), (1, 1)))

        loop(16, self_part)

        halo_d.wait_recv()

        def flip(index):
            a, c = index // 4, index % 4
            raw[e, a, c + 1, 2] = raw[e, a, c + 1, 2] * mirror

        loop(16, flip)
        halo_cm.start()
        halo_cp.start()

        def prepare_above(index):
            prepare_right(e, index // 4, index % 4 + 1, 2)

        loop(16, prepare_above)

        def above_part(index):
            a, c = index // 2, index % 2 + 2 * di
            tiles(a * 4 + c, a, c, a, c + 1, 4, 12, 0.0, ((2, (0,), (0,)),))

        loop(8, above_part)

        def pair_part(it):
            @pl.when(it == 12)
            def _():
                halo_cm.wait_recv()
                halo_cp.wait_recv()
                halo_a.start()

            @pl.when(it == 24)
            def _():
                halo_a.wait_recv()

                def side(index):
                    for layer in range(3):
                        prepare_right(e, index, 5, layer)

                def front(index):
                    for layer in range(3):
                        prepare_right(e, 4, index, layer)

                loop(4, side)
                loop(6, front)

            @pl.when(it == 46)
            def _():
                def give(index):
                    for layer in range(3):
                        net[e, 4, index, layer] = reduced(4, index, layer)

                loop(6, give)
                back_a.start()

            @pl.when(it == 55)
            def _():
                back_a.wait_recv()
                for layer in range(3):
                    net[e, 0, 0, layer] = reduced(0, 0, layer) + in_a[e, 0, layer]

                def give(index):
                    for layer in range(3):
                        net[e, index, 5, layer] = reduced(index, 5, layer)

                loop(4, give)
                for layer in range(3):
                    net[e, 0, 5, layer] += in_a[e, 5, layer]
                back_cp.start()
                back_cm.start()

            def pick(values, default):
                for limit, value in reversed(values):
                    default = jnp.where(it < limit, value, default)
                return default

            a = pick(
                ((12, it // 3), (24, (it - 12) // 4), (28, it - 24), (31, it - 28), (34, it - 30), (46, 3),
                 (55, (it - 46) // 3)), (it - 55) // 3)
            c = pick(
                ((12, it % 3), (24, it % 4), (34, 3), (46, (it - 34) % 4), (55, (it - 46) % 3)), 1 + (it - 55) % 3)
            oa = pick(((12, 0), (24, 1), (28, 0), (31, 1), (34, -1)), 1)
            oc = pick(((12, 1), (24, 0), (34, 1), (38, 0), (42, 1), (46, -1), (55, 1)), -1)
            base = (oa + 1) * 9 + (oc + 1) * 3
            entry = (oa + 1) * 3 + oc + 1
            shift = jnp.where(row_id == 0, oa.astype(F32), jnp.where(row_id == 1, oc.astype(F32), 0.0))
            tiles(a * 4 + c, a, c, a + oa, c + 1 + oc, entry, base, shift,
                  ((0, (0, 1), (0, 1)), (1, (0, 1), (0, 1)), (2, (0,), (0,))))

        loop(64, pair_part)

        back_cp.wait_recv()
        back_cm.wait_recv()

        def give_above(index):
            a, c = index // 4, index % 4
            net[e, a, c + 1, 2] = reduced(a, c + 1, 2)

        loop(16, give_above)
        for c in range(4):
            net[e, 0, c + 1, 2] += in_a[e, c + 1, 2]
        for a in range(4):
            net[e, a, 1, 2] += in_cp[e, a, 2]
        net[e, 0, 4, 2] += in_cm[e, 2]
        back_d.start()

        def collect(index):
            a, c = index // 4, index % 4
            for layer in (0, 1):
                sums = [acc_l[index, k, layer * W : layer * W + W] for k in range(4)]
                sums = [x + pltpu.roll(x, 64, 1) for x in sums]
                pairs = [jnp.where(lane_id < 64, sums[0], sums[1]), jnp.where(lane_id < 64, sums[2], sums[3])]
                pairs = [x + pltpu.roll(x, turn, 1) for x, turn in zip(pairs, (96, 32))]
                turned = jnp.where(lane_id % 64 < 32, pairs[0], pairs[1]).T
                lines = [jnp.sum(fold(turned[start : start + 32]), 0, keepdims=True) for start in (0, 64, 32, 96)]
                left = jnp.concatenate(
                    [jnp.zeros((3, W), F32), -lines[0], -lines[1], -lines[2], lines[3], jnp.zeros((1, W), F32)], 0)
                own[a, c, layer] = left + reduced(a, c + 1, layer)

        loop(16, collect)
        for c in range(4):
            for layer in (0, 1):
                own[0, c, layer] += in_a[e, c + 1, layer]
        for a in range(4):
            for layer in (0, 1):
                own[a, 0, layer] += in_cp[e, a, layer]
        for layer in (0, 1):
            own[0, 3, layer] += in_cm[e, layer]
        back_d.wait_recv()

        def finish(index):
            a, c = index // 4, index % 4
            for layer in (0, 1):
                state = raw[0, a, c + 1, layer]
                total = own[a, c, layer]
                if layer == 0:
                    total = total + in_d[e, a, c] * mirror
                rate = total * (-KERNEL / state[7:8]) + gravity
                speed = state + HALF * rate
                keep = (row_id >= 3) & (row_id < 7)

                @pl.when(e == 0)
                def _():
                    moved_place = state + HALF * pltpu.roll(state, 5, 0)
                    raw[1, a, c + 1, layer] = jnp.where(keep, speed, jnp.where(row_id < 3, moved_place, state))

                @pl.when(e == 1)
                def _():
                    at = pl.ds(depth_of(layer), 1)
                    start = jnp.where(row_id == 2, state * sign, state)
                    start = jnp.where(row_id < 3, start + 0.5, start)
                    start = jnp.where(row_id == 5, start * sign, start)
                    rate_g = jnp.where(row_id == 5, rate * sign, rate)
                    corr = start + HALF * rate_g
                    place = start + HALF * pltpu.roll(corr, 5, 0)
                    new = jnp.where(row_id < 3, 2.0 * place - start, 2.0 * corr - start)
                    for k in range(7):
                        adv[k, a, c, at, :] = new[k : k + 1]
                    rates[0, a, c, at, :] = rate_g[6:7]
                    for k in range(3):
                        rates[k + 1, a, c, at, :] = rate_g[3 + k : 4 + k]

        loop(16, finish)
        for item in (halo_d, halo_cm, halo_cp, halo_a, back_a, back_cp, back_cm, back_d):
            item.wait_send()

    loop(2, evaluate)


def shards(counts, offsets, velocity, density, mass, pairs):
    table = jnp.asarray(shift_table(), BF16)
    vmem = pl.BlockSpec(memory_space=pltpu.VMEM)
    smem = pl.BlockSpec(memory_space=pltpu.SMEM)

    def body(*refs):
        step_kernel(counts, *refs)

    return pl.pallas_call(
        body,
        out_shape=(
            jax.ShapeDtypeStruct((4, 4, 4, 2, W), F32),
            jax.ShapeDtypeStruct((7, 4, 4, 2, W), F32),
        ),
        in_specs=[vmem, vmem, vmem, vmem, smem, vmem],
        out_specs=(vmem, vmem),
        scratch_shapes=[
            pltpu.VMEM((2, 5, 6, 3, 8, W), F32),
            pltpu.VMEM((5, 6, 3, 32, 2 * W), BF16),
            pltpu.VMEM((5, 6, 3, 32, W), BF16),
            pltpu.VMEM((5, 6, 3, 8, W), F32),
            pltpu.VMEM((16, 2 * W, W), BF16),
            pltpu.VMEM((16, 2 * W, W), F32),
            pltpu.VMEM((16, 4, 2 * W, W), F32),
            pltpu.VMEM((5, 6, 3, 4, 8, W), F32),
            pltpu.VMEM((2, 5, 6, 3, 8, W), F32),
            pltpu.VMEM((4, 4, 2, 8, W), F32),
            pltpu.VMEM((2, 6, 3, 8, W), F32),
            pltpu.VMEM((2, 4, 3, 8, W), F32),
            pltpu.VMEM((2, 3, 8, W), F32),
            pltpu.VMEM((2, 4, 4, 8, W), F32),
            pltpu.SemaphoreType.DMA((2, 8)),
            pltpu.SemaphoreType.DMA((2, 8)),
        ],
        compiler_params=pltpu.CompilerParams(
            collective_id=0, has_side_effects=True, vmem_limit_bytes=40 * 1024 * 1024
        ),
        name="sph_step",
    )(offsets, velocity, density, mass, pairs.reshape(-1), table)


def solution(mesh):
    counts = (mesh.shape["along"], mesh.shape["cross"])

    def run(*args):
        return shards(counts, *args)

    spec = P(None, "along", "cross", "depth", None)
    plain = P("along", "cross", "depth", None)
    return jax.shard_map(
        run,
        mesh=mesh,
        in_specs=(spec, spec, plain, plain, P(None, "along", "cross", "depth")),
        out_specs=(spec, spec),
        check_vma=False,
    )
```

time: 578 us -> 168 us (0.29)
  other arithmetic: 264 us -> 0 us
  starting transfers between devices: 172 us -> 0 us
  Pallas kernels: 0 us -> 162 us
  local copies, waits for them, and re-layouts: 107 us -> 4.57 us
  waiting for transfers between devices: 27.9 us -> 0 us
    reduce_sum x20 -> x0, other arithmetic: 181 us -> none  [pair_terms(): jnp.sum(flux_term * mass_left, -2)]
    ppermute x24 -> x0, starting transfers between devices: 172 us -> none  [the longest x12 100 us: with_halo(): lax.ppermute(head, axis, [((i + 1) % count, i) for i in range(ends)])]
    pallas_call x0 -> x1, Pallas kernels: none -> 162 us  [shards(): pl.pallas_call(body, out_shape=(jax.ShapeDtypeStruct((4, 4, 4, 2, W), F32...]
    gather x141 -> x0, local copies, waits for them, and re-layouts: 95.4 us -> none  [the longest x20 14.3 us: one_turn(): side_table[chosen][:, None, None]]
    scatter-add x48 -> x0, other arithmetic: 67.8 us -> none  [the longest x20 34.4 us: one_turn(): accumulated = accumulated.at[left_ids].add(weight * left_rates)]
    ppermute x24 -> x0, waiting for transfers between devices: 27.9 us -> none  [the longest x12 27.8 us: with_halo(): lax.ppermute(head, axis, [((i + 1) % count, i) for i in range(ends)])]
    slice x78 -> x0, local copies, waits for them, and re-layouts: 7.98 us -> none  [the longest x20 3.52 us: pair_terms(): shift_vec[..., component, None, None]]
  transfers between devices with their start and end apart: 24 -> 0, of which waited for: 11 -> 0; matrix products, arithmetic and copies ran while one was open for 1% -> 0% of each run, Pallas kernels for 0% -> 0%
where the time goes in v1:
time: 168 us; the launch traced here: 167 us
  Pallas kernels  162 us (96%)
  local copies, waits for them, and re-layouts  4.57 us (3%)
    pallas_call x1, Pallas kernels, shards(): pl.pallas_call(body, out_shape=(jax.ShapeDtypeStruct((4, 4, 4, 2, W), F32...  162 us
    unnamed x13, local copies, waits for them, and re-layouts  4.36 us

profile of v1, /device:TPU:1, one launch (start us, length us, event | category | flops | bytes accessed | tf_op | source)
XLA Modules:
  0.0 167.4 jit_solution(13016015645925672492)
XLA Ops:
  0.6 0.0 copy-start
  0.6 1.0 copy.8
  1.6 0.0 copy-start.1
  1.6 0.0 copy-start.3
  1.6 0.2 reshape.7.refs_4_
  1.9 0.0 copy-done
  1.9 0.6 copy-done.1
  2.4 0.0 copy-done.3
  2.4 0.0 copy-start.2
  2.4 0.8 copy-done.2
  3.2 0.0 copy-start.4
  3.2 0.7 copy-done.4
  3.9 162.2 %sph_step.1 = (f32[4,4,4,2,128]{4,3,2,1,0:T(2,128)S(1)}, f32[7,4,4,2,128]{4,3,2,1,0:T(2,128)S(1)}) custom-call(f32[3,4,4,2,128]{4,3,2,1,0:T(2,128)S(1)} %copy-done.1, f32[3,4,4,2,128]{4,3,2,1,0:T(2,128)S(1)} %copy-done.2, f32[4,4,2,128]{3,2,1,0:T(2,128)S(1)} %copy-done.3, f32[4,4,2,128]{3,2,1,0:T(2,128)S(1)} %copy-done.4, s32[832]{0:T(1024)S(1)} %reshape.7.refs_4_, ...), custom_call_target="tpu_custom_call" | custom-call | tf_op jit(solution)/shard_map/sph_step/pallas_call | solution.py:442
  166.1 0.6 copy.11
  166.8 0.6 copy.12
Async XLA Ops:
  0.6 1.2 copy-start
  1.6 0.8 copy-start.1
  1.6 0.8 copy-start.3
  2.4 0.8 copy-start.2
  3.2 0.7 copy-start.4

commit v2 on v1

--- a/solution.py
+++ b/solution.py
@@ -22,23 +22,20 @@
 BF16 = jnp.bfloat16
 W = 128
 CHUNK = 32
-
-
-def shift_table():
-    table = np.zeros((9, 80, 2 * W), np.float32)
-    for oa in (-1, 0, 1):
-        for oc in (-1, 0, 1):
-            entry = table[(oa + 1) * 3 + oc + 1]
-            for start in (0, 8, 16):
-                entry[start : start + 2, :W] = [[2 * oa], [2 * oc]]
-                entry[start + 6, :W] = 1
-                entry[start + 3 : start + 5, W:] = [[oa], [oc]]
-                entry[start + 7, W:] = 1
-            for start in (24, 32, 40):
-                entry[start : start + 2, :W] = [[-2 * oa], [-2 * oc]]
-                entry[start + 3 : start + 5, W:] = [[-oa], [-oc]]
-            entry[48, :W] = oa * oa + oc * oc
-    return table
+CENTRE = 4
+
+
+def shift_rows(oa, oc):
+    row = lax.broadcasted_iota(jnp.int32, (80, 2 * W), 0)
+    near = lax.broadcasted_iota(jnp.int32, (80, 2 * W), 1) < W
+    part = row % 8
+    scale = jnp.where(near, 2.0, 1.0) * jnp.where(row < 24, 1.0, -1.0)
+    first = jnp.where(near, 0, 3)
+    one = jnp.where(near, 6, 7)
+    value = jnp.where(part == first, oa * scale, jnp.where(part == first + 1, oc * scale, 0.0))
+    value = jnp.where((part == one) & (row < 24), 1.0, value)
+    last = jnp.where((row == 48) & near, oa * oa + oc * oc, 0.0)
+    return jnp.where(row < 48, value, last).astype(BF16)
 
 
 def split3(value):
@@ -101,8 +98,8 @@
 
 
 def step_kernel(
-    counts, off, vel, den, mas, flags, table, rates, adv,
-    raw, fixed, moved, plain, lefts, cols, acc_l, acc_r, net, own,
+    counts, off, vel, den, mas, flags, rates, adv,
+    table, shifts, spread, picks, ready, raw, fixed, moved, plain, lefts, cols, acc_l, acc_r, net, own,
     in_a, in_cp, in_cm, in_d, send_sem, recv_sem,
 ):
     ai = lax.axis_index("along")
@@ -153,54 +150,60 @@
         moments, flat = derive(raw[e, a, c, layer], layer)
         parts = split3(moments)
         solid, loose = right_tiles(parts)
-        fixed[a, c, layer] = solid
-        moved[a, c, layer] = loose
-        plain[a, c, layer] = flat
+        slot = (a * 6 + c) * 3 + layer
+        fixed[slot] = solid
+        moved[slot] = loose
+        plain[slot] = flat
         return parts, flat
 
     def prepare_own(e, a, c):
+        one = jnp.ones((8, W), F32)
         for layer in (0, 1):
             parts, flat = prepare_right(e, a, c + 1, layer)
             d0, d1, d2 = parts
-            one = jnp.ones((8, W), F32)
-            stack = jnp.concatenate(
-                [d0, d0, d1, d1, d0, d2, one, one, one, d0, d1, d2, one, zero8, zero8, flat], 0
-            )
-            turned = stack.T
-            lefts[a * 4 + c, layer * W : layer * W + W] = turned.astype(BF16)
-            cols[a * 4 + c, layer * W : layer * W + W] = turned
-
-    def right_side(entry, a, c, layer):
-        solid = fixed[a, c, layer]
-        loose = moved[a, c, layer]
+            f0, f1, f2 = split3(flat)
+            stack = jnp.concatenate([d0, d0, d1, d1, d0, d2, one, one, one, d0, d1, d2, one, f0, f1, f2], 0)
+            lefts[a * 4 + c, layer * W : layer * W + W] = stack.T.astype(BF16)
+        wide = jnp.dot(lefts[a * 4 + c], spread[...], preferred_element_type=F32)
+        for k in range(6):
+            cols[a * 4 + c, k] = wide[:, k * W : k * W + W]
+
+    def right_side(entry, slot):
+        solid = fixed[slot]
+        loose = moved[slot]
         bent = jnp.concatenate([loose, loose], 1) * table[entry, 0:32]
         return jnp.concatenate([solid[0:16], solid[0:16], solid[16:32], bent, table[entry, 32:80]], 0)
 
-    def flag_of(base, a, c, layer, right_layer):
+    def flag_place(layer, right_layer):
         step = (1, 0, 2)[right_layer] - (1, 0, 2)[layer]
-        skipped = (1 + (1 - 2 * di) * step) // 2 if isinstance(base, int) else base // 13
-        listed = base + 1 + (1 - 2 * di) * step - skipped
-        return flags[listed * 32 + (a * 4 + c) * 2 + depth_of(layer)].astype(F32)
-
-    def tiles(p, a, c, qa, qc, entry, base, shift, work, first=False, own_pairs=()):
+        return (1 - 2 * di) * step * 32 + depth_of(layer)
+
+    places = {pair: flag_place(*pair) for pair in ((0, 0), (0, 1), (0, 2), (1, 0), (1, 1))}
+
+    def tiles(p, q, entry, core, work, first=False, own_pairs=(), follow=None):
         left_total = {}
         for right_layer, left_layers, both in work:
             lo, hi = min(left_layers), max(left_layers) + 1
-            product = jnp.dot(
-                lefts[p, lo * W : hi * W], right_side(entry, qa, qc, right_layer), preferred_element_type=F32
-            )
-            flat = plain[qa, qc, right_layer]
-            placed = flat + shift
+            product = None
+            if follow is None:
+                product = jnp.dot(
+                    lefts[p, lo * W : hi * W], right_side(entry, q + right_layer), preferred_element_type=F32
+                )
+            flat = plain[q + right_layer]
+            placed = flat if entry is CENTRE else flat + shifts[entry]
             rows = [placed[k : k + 1] for k in range(5)]
             right_total = None
             for layer in left_layers:
                 mass_row = flat[5:6]
                 if (layer, right_layer) not in own_pairs:
-                    mass_row = mass_row * flag_of(base, a, c, layer, right_layer)
+                    mass_row = mass_row * flags[core + places[layer, right_layer]].astype(F32)
                 for start in range(0, W, CHUNK):
                     spot = layer * W + start
-                    here = product[spot - lo * W : spot - lo * W + CHUNK]
-                    col = [cols[p, spot : spot + CHUNK, 120 + k : 121 + k] for k in range(6)]
+                    if product is None:
+                        here = ready[right_layer * 2 * W + spot : right_layer * 2 * W + spot + CHUNK]
+                    else:
+                        here = product[spot - lo * W : spot - lo * W + CHUNK]
+                    col = [cols[p, k, spot : spot + CHUNK] for k in range(6)]
                     terms = pair_chunk(here[:, :W], here[:, W:], col, rows, mass_row)
                     key = spot
                     if key in left_total:
@@ -212,7 +215,9 @@
                         right_total = folded if right_total is None else [x + y for x, y in zip(right_total, folded)]
             if right_total is not None:
                 for k in range(4):
-                    acc_r[qa, qc, right_layer, k] += right_total[k]
+                    acc_r[q + right_layer, k] += right_total[k]
+        if follow is not None:
+            follow()
         for spot, terms in left_total.items():
             for k in range(4):
                 if first:
@@ -221,7 +226,8 @@
                     acc_l[p, k, spot : spot + CHUNK] += terms[k]
 
     def reduced(a, c, layer):
-        terms = [jnp.sum(acc_r[a, c, layer, k], 0, keepdims=True) for k in range(4)]
+        slot = (a * 6 + c) * 3 + layer
+        terms = [jnp.sum(acc_r[slot, k], 0, keepdims=True) for k in range(4)]
         return jnp.concatenate([jnp.zeros((3, W), F32)] + terms + [jnp.zeros((1, W), F32)], 0)
 
     def loop(count, body):
@@ -240,6 +246,19 @@
             lines[5] = lines[5] * sign
             raw[0, a, c + 1, layer] = jnp.concatenate(lines, 0)
 
+    def fill_table(index):
+        oa, oc = (index // 3 - 1).astype(F32), (index % 3 - 1).astype(F32)
+        table[index] = shift_rows(oa, oc)
+        shifts[index] = jnp.where(row_id == 0, oa, jnp.where(row_id == 1, oc, 0.0))
+
+    loop(9, fill_table)
+    feature = lax.broadcasted_iota(jnp.int32, (W, W), 0)
+    for k in range(6):
+        spread[:, k * W : k * W + W] = jnp.where((feature >= 104) & (feature % 8 == k), 1.0, 0.0).astype(BF16)
+    pick_row = lax.broadcasted_iota(jnp.int32, (16, 2 * W), 0)
+    upper = lax.broadcasted_iota(jnp.int32, (16, 2 * W), 1) % W // 64
+    picks[0] = jnp.where(pick_row == 3 + upper, -1.0, 0.0).astype(BF16)
+    picks[1] = jnp.where(pick_row == 5 + upper, jnp.where(upper == 0, -1.0, 1.0), 0.0).astype(BF16)
     loop(16, fill)
 
     def evaluate(e):
@@ -247,23 +266,17 @@
         halo_d.start()
 
         def first_part(index):
-            prepare_own(e, index // 4, index % 4)
-
-        loop(16, first_part)
+            for c in (0, 1):
+                prepare_own(e, index // 2, index % 2 * 2 + c)
+
+        loop(8, first_part)
 
         def clear(index):
-            for c in range(6):
-                for layer in range(3):
-                    for k in range(4):
-                        acc_r[index, c, layer, k] = zero8
+            for number in range(18):
+                for k in range(4):
+                    acc_r[index * 18 + number, k] = zero8
 
         loop(5, clear)
-
-        def self_part(index):
-            a, c = index // 4, index % 4
-            tiles(index, a, c, a, c + 1, 4, 12, 0.0, ((0, (0, 1), (1,)), (1, (1,), ())), True, ((0, 0), (1, 1)))
-
-        loop(16, self_part)
 
         halo_d.wait_recv()
 
@@ -280,20 +293,58 @@
 
         loop(16, prepare_above)
 
-        def above_part(index):
-            a, c = index // 2, index % 2 + 2 * di
-            tiles(a * 4 + c, a, c, a, c + 1, 4, 12, 0.0, ((2, (0,), (0,)),))
-
-        loop(8, above_part)
-
-        def pair_part(it):
-            @pl.when(it == 12)
+        def column_part(index):
+            a = index // 2
+
+            def where_is(c):
+                return a * 4 + c, (a * 6 + c + 1) * 3, (13 - di) * 32 - (1 - 2 * di) * 32 + (a * 4 + c) * 2
+
+            for c in (index % 2, index % 2 + 2):
+                p, q, core = where_is(c)
+                tiles(p, q, CENTRE, core, ((0, (0, 1), (1,)), (1, (1,), ())), True, ((0, 0), (1, 1)))
+            p, q, core = where_is(index % 2 + 2 * di)
+            tiles(p, q, CENTRE, core, ((2, (0,), (0,)),))
+
+        loop(8, column_part)
+
+        def pick(values, default, at):
+            for limit, value in reversed(values):
+                default = jnp.where(at < limit, value, default)
+            return default
+
+        def locate(it):
+            a = pick(
+                ((12, it // 3), (24, (it - 12) // 4), (28, it - 24), (31, it - 28), (34, it - 30), (46, 3),
+                 (55, (it - 46) // 3)), (it - 55) // 3, it)
+            c = pick(
+                ((12, it % 3), (24, it % 4), (34, 3), (46, (it - 34) % 4), (55, (it - 46) % 3)), 1 + (it - 55) % 3, it)
+            oa = pick(((12, 0), (24, 1), (28, 0), (31, 1), (34, -1)), 1, it)
+            oc = pick(((12, 1), (24, 0), (34, 1), (38, 0), (42, 1), (46, -1), (55, 1)), -1, it)
+            base = (oa + 1) * 9 + (oc + 1) * 3
+            core = (base + 1 - base // 13) * 32 + (a * 4 + c) * 2
+            return a * 4 + c, ((a + oa) * 6 + c + 1 + oc) * 3, (oa + 1) * 3 + oc + 1, core
+
+        def lead(place):
+            p, q, entry, core = place
+            for layer, rows in ((0, 2 * W), (1, 2 * W), (2, W)):
+                ready[layer * 2 * W : layer * 2 * W + rows] = jnp.dot(
+                    lefts[p, 0:rows], right_side(entry, q + layer), preferred_element_type=F32
+                )
+
+        def pair_part(it, carry):
+            place, following = carry
+            tiles(*place, ((0, (0, 1), (0, 1)), (1, (0, 1), (0, 1)), (2, (0,), (0,))), follow=lambda: lead(following))
+            return following, locate(lax.rem(it + 2, 64))
+
+        def phase_part(phase, carry):
+
+            @pl.when(phase == 1)
             def _():
                 halo_cm.wait_recv()
                 halo_cp.wait_recv()
                 halo_a.start()
 
-            @pl.when(it == 24)
+            @pl.when(phase == 2)
             def _():
                 halo_a.wait_recv()
 
@@ -308,7 +359,7 @@
                 loop(4, side)
                 loop(6, front)
 
-            @pl.when(it == 46)
+            @pl.when(phase == 3)
             def _():
                 def give(index):
                     for layer in range(3):
@@ -317,7 +368,7 @@
                 loop(6, give)
                 back_a.start()
 
-            @pl.when(it == 55)
+            @pl.when(phase == 4)
             def _():
                 back_a.wait_recv()
                 for layer in range(3):
@@ -333,25 +384,13 @@
                 back_cp.start()
                 back_cm.start()
 
-            def pick(values, default):
-                for limit, value in reversed(values):
-                    default = jnp.where(it < limit, value, default)
-                return default
-
-            a = pick(
-                ((12, it // 3), (24, (it - 12) // 4), (28, it - 24), (31, it - 28), (34, it - 30), (46, 3),
-                 (55, (it - 46) // 3)), (it - 55) // 3)
-            c = pick(
-                ((12, it % 3), (24, it % 4), (34, 3), (46, (it - 34) % 4), (55, (it - 46) % 3)), 1 + (it - 55) % 3)
-            oa = pick(((12, 0), (24, 1), (28, 0), (31, 1), (34, -1)), 1)
-            oc = pick(((12, 1), (24, 0), (34, 1), (38, 0), (42, 1), (46, -1), (55, 1)), -1)
-            base = (oa + 1) * 9 + (oc + 1) * 3
-            entry = (oa + 1) * 3 + oc + 1
-            shift = jnp.where(row_id == 0, oa.astype(F32), jnp.where(row_id == 1, oc.astype(F32), 0.0))
-            tiles(a * 4 + c, a, c, a + oa, c + 1 + oc, entry, base, shift,
-                  ((0, (0, 1), (0, 1)), (1, (0, 1), (0, 1)), (2, (0,), (0,))))
-
-        loop(64, pair_part)
+            start, stop = (pick(((1, x), (2, y), (3, z), (4, w)), v, phase) for x, y, z, w, v in zip(
+                (0, 11), (11, 23), (23, 46), (46, 55), (55, 64)))
+            return lax.fori_loop(start, stop, pair_part, carry)
+
+        begin = locate(jnp.int32(0))
+        lead(begin)
+        lax.fori_loop(0, 5, phase_part, (begin, locate(jnp.int32(1))))
 
         back_cp.wait_recv()
         back_cm.wait_recv()
@@ -368,20 +407,28 @@
         net[e, 0, 4, 2] += in_cm[e, 2]
         back_d.start()
 
-        def collect(index):
-            a, c = index // 4, index % 4
-            for layer in (0, 1):
-                sums = [acc_l[index, k, layer * W : layer * W + W] for k in range(4)]
-                sums = [x + pltpu.roll(x, 64, 1) for x in sums]
-                pairs = [jnp.where(lane_id < 64, sums[0], sums[1]), jnp.where(lane_id < 64, sums[2], sums[3])]
-                pairs = [x + pltpu.roll(x, turn, 1) for x, turn in zip(pairs, (96, 32))]
-                turned = jnp.where(lane_id % 64 < 32, pairs[0], pairs[1]).T
-                lines = [jnp.sum(fold(turned[start : start + 32]), 0, keepdims=True) for start in (0, 64, 32, 96)]
-                left = jnp.concatenate(
-                    [jnp.zeros((3, W), F32), -lines[0], -lines[1], -lines[2], lines[3], jnp.zeros((1, W), F32)], 0)
-                own[a, c, layer] = left + reduced(a, c + 1, layer)
-
-        loop(16, collect)
+        def collect(number):
+            for index in (number * 2, number * 2 + 1):
+                a, c = index // 4, index % 4
+                halves = [[], []]
+                for layer in (0, 1):
+                    sums = [acc_l[index, k, layer * W : layer * W + W] for k in range(4)]
+                    low = lane_id < 64
+                    for half, (x, y) in zip(halves, (sums[0:2], sums[2:4])):
+                        both = jnp.where(low, x, y) + pltpu.roll(jnp.where(low, y, x), 64, 1)
+                        top = both.astype(BF16)
+                        half.append(jnp.concatenate([top, (both - top.astype(F32)).astype(BF16)], 1))
+                left = None
+                for number_of_half, half in enumerate(halves):
+                    part = lax.dot_general(
+                        picks[number_of_half], jnp.concatenate(half, 0), (((1,), (1,)), ((), ())),
+                        preferred_element_type=F32,
+                    )
+                    left = part if left is None else left + part
+                for layer in (0, 1):
+                    own[a, c, layer] = left[0:8, layer * W : layer * W + W] + reduced(a, c + 1, layer)
+
+        loop(8, collect)
         for c in range(4):
             for layer in (0, 1):
                 own[0, c, layer] += in_a[e, c + 1, layer]
@@ -432,7 +479,6 @@
 
 
 def shards(counts, offsets, velocity, density, mass, pairs):
-    table = jnp.asarray(shift_table(), BF16)
     vmem = pl.BlockSpec(memory_space=pltpu.VMEM)
     smem = pl.BlockSpec(memory_space=pltpu.SMEM)
 
@@ -445,17 +491,22 @@
             jax.ShapeDtypeStruct((4, 4, 4, 2, W), F32),
             jax.ShapeDtypeStruct((7, 4, 4, 2, W), F32),
         ),
-        in_specs=[vmem, vmem, vmem, vmem, smem, vmem],
+        in_specs=[vmem, vmem, vmem, vmem, smem],
         out_specs=(vmem, vmem),
         scratch_shapes=[
+            pltpu.VMEM((9, 80, 2 * W), BF16),
+            pltpu.VMEM((9, 8, W), F32),
+            pltpu.VMEM((W, 6 * W), BF16),
+            pltpu.VMEM((2, 16, 2 * W), BF16),
+            pltpu.VMEM((5 * W, 2 * W), F32),
             pltpu.VMEM((2, 5, 6, 3, 8, W), F32),
-            pltpu.VMEM((5, 6, 3, 32, 2 * W), BF16),
-            pltpu.VMEM((5, 6, 3, 32, W), BF16),
-            pltpu.VMEM((5, 6, 3, 8, W), F32),
+            pltpu.VMEM((90, 32, 2 * W), BF16),
+            pltpu.VMEM((90, 32, W), BF16),
+            pltpu.VMEM((90, 8, W), F32),
             pltpu.VMEM((16, 2 * W, W), BF16),
-            pltpu.VMEM((16, 2 * W, W), F32),
+            pltpu.VMEM((16, 6, 2 * W, W), F32),
             pltpu.VMEM((16, 4, 2 * W, W), F32),
-            pltpu.VMEM((5, 6, 3, 4, 8, W), F32),
+            pltpu.VMEM((90, 4, 8, W), F32),
             pltpu.VMEM((2, 5, 6, 3, 8, W), F32),
             pltpu.VMEM((4, 4, 2, 8, W), F32),
             pltpu.VMEM((2, 6, 3, 8, W), F32),
@@ -469,7 +520,7 @@
             collective_id=0, has_side_effects=True, vmem_limit_bytes=40 * 1024 * 1024
         ),
         name="sph_step",
-    )(offsets, velocity, density, mass, pairs.reshape(-1), table)
+    )(offsets, velocity, density, mass, pairs.reshape(-1))
 
 
 def solution(mesh):

time: 168 us -> 108 us (0.64)
  Pallas kernels: 162 us -> 104 us
    pallas_call x1, Pallas kernels: 162 us -> 104 us  [shards(): pl.pallas_call(body, out_shape=(jax.ShapeDtypeStruct((4, 4, 4, 2, W), F32...]
    unnamed x13 -> x11, local copies, waits for them, and re-layouts: 4.36 us -> 2.81 us
where the time goes in v2:
time: 108 us
  Pallas kernels  104 us (96%)
  local copies, waits for them, and re-layouts  3.01 us (3%)
    pallas_call x1, Pallas kernels, shards(): pl.pallas_call(body, out_shape=(jax.ShapeDtypeStruct((4, 4, 4, 2, W), F32...  104 us
    unnamed x11, local copies, waits for them, and re-layouts  2.81 us

profile of v2, /device:TPU:1, one launch (start us, length us, event | category | flops | bytes accessed | tf_op | source)
XLA Modules:
  0.0 108.0 jit_solution(4430221264864404415)
XLA Ops:
  0.6 0.9 copy.7
  1.6 0.0 copy-start
  1.6 0.0 copy-start.1
  1.6 0.0 copy-start.2
  1.6 0.0 copy-start.3
  1.6 0.2 reshape.7.refs_4_
  1.8 0.6 copy-done
  2.4 0.0 copy-done.1
  2.4 0.0 copy-done.2
  2.4 0.0 copy-done.3
  2.4 104.3 %sph_step.1 = (f32[4,4,4,2,128]{4,3,2,1,0:T(2,128)S(1)}, f32[7,4,4,2,128]{4,3,2,1,0:T(2,128)S(1)}) custom-call(f32[3,4,4,2,128]{4,3,2,1,0:T(2,128)S(1)} %copy-done, f32[3,4,4,2,128]{4,3,2,1,0:T(2,128)S(1)} %copy-done.1, f32[4,4,2,128]{3,2,1,0:T(2,128)S(1)} %copy-done.2, f32[4,4,2,128]{3,2,1,0:T(2,128)S(1)} %copy-done.3, s32[832]{0:T(1024)S(1)} %reshape.7.refs_4_), custom_call_target="tpu_custom_call" | custom-call | tf_op jit(solution)/shard_map/sph_step/pallas_call | solution.py:488
  106.7 0.6 copy.10
  107.4 0.6 copy.11
Async XLA Ops:
  1.6 0.8 copy-start
  1.6 0.8 copy-start.1
  1.6 0.8 copy-start.2
  1.6 0.8 copy-start.3

commit v3 on v2

--- a/solution.py
+++ b/solution.py
@@ -21,7 +21,7 @@
 F32 = jnp.float32
 BF16 = jnp.bfloat16
 W = 128
-CHUNK = 32
+CHUNK = 8
 CENTRE = 4
 
 
@@ -180,51 +180,54 @@
 
     places = {pair: flag_place(*pair) for pair in ((0, 0), (0, 1), (0, 2), (1, 0), (1, 1))}
 
-    def tiles(p, q, entry, core, work, first=False, own_pairs=(), follow=None):
-        left_total = {}
-        for right_layer, left_layers, both in work:
-            lo, hi = min(left_layers), max(left_layers) + 1
-            product = None
-            if follow is None:
-                product = jnp.dot(
+    def tiles(p, q, entry, core, work, first=False, own_pairs=(), buffer=None):
+        products = {}
+        if buffer is None:
+            for right_layer, left_layers, both in work:
+                lo, hi = min(left_layers), max(left_layers) + 1
+                products[right_layer] = lo, jnp.dot(
                     lefts[p, lo * W : hi * W], right_side(entry, q + right_layer), preferred_element_type=F32
                 )
+        rows, masses = {}, {}
+        for right_layer, left_layers, both in work:
             flat = plain[q + right_layer]
             placed = flat if entry is CENTRE else flat + shifts[entry]
-            rows = [placed[k : k + 1] for k in range(5)]
-            right_total = None
+            rows[right_layer] = [placed[k : k + 1] for k in range(5)]
             for layer in left_layers:
                 mass_row = flat[5:6]
                 if (layer, right_layer) not in own_pairs:
                     mass_row = mass_row * flags[core + places[layer, right_layer]].astype(F32)
-                for start in range(0, W, CHUNK):
-                    spot = layer * W + start
-                    if product is None:
-                        here = ready[right_layer * 2 * W + spot : right_layer * 2 * W + spot + CHUNK]
+                masses[layer, right_layer] = mass_row
+        right_total = {}
+        for layer in (0, 1):
+            if not any(layer in left_layers for _, left_layers, _ in work):
+                continue
+            for start in range(0, W, CHUNK):
+                spot = layer * W + start
+                col = [cols[p, k, spot : spot + CHUNK] for k in range(6)]
+                left_total = None
+                for right_layer, left_layers, both in work:
+                    if layer not in left_layers:
+                        continue
+                    if buffer is None:
+                        lo, product = products[right_layer]
+                        here = product[spot - lo * W : spot - lo * W + CHUNK]
                     else:
-                        here = product[spot - lo * W : spot - lo * W + CHUNK]
-                    col = [cols[p, k, spot : spot + CHUNK] for k in range(6)]
-                    terms = pair_chunk(here[:, :W], here[:, W:], col, rows, mass_row)
-                    key = spot
-                    if key in left_total:
-                        left_total[key] = [x + y for x, y in zip(left_total[key], terms)]
-                    else:
-                        left_total[key] = terms
+                        here = ready[buffer, right_layer * 2 * W + spot : right_layer * 2 * W + spot + CHUNK]
+                    terms = pair_chunk(here[:, :W], here[:, W:], col, rows[right_layer], masses[layer, right_layer])
+                    left_total = terms if left_total is None else [x + y for x, y in zip(left_total, terms)]
                     if layer in both:
                         folded = [fold(x) for x in terms]
-                        right_total = folded if right_total is None else [x + y for x, y in zip(right_total, folded)]
-            if right_total is not None:
+                        old = right_total.get(right_layer)
+                        right_total[right_layer] = folded if old is None else [x + y for x, y in zip(old, folded)]
                 for k in range(4):
-                    acc_r[q + right_layer, k] += right_total[k]
-        if follow is not None:
-            follow()
-        for spot, terms in left_total.items():
+                    if first:
+                        acc_l[p, k, spot : spot + CHUNK] = left_total[k]
+                    else:
+                        acc_l[p, k, spot : spot + CHUNK] += left_total[k]
+        for right_layer, total in right_total.items():
             for k in range(4):
-                if first:
-                    acc_l[p, k, spot : spot + CHUNK] = terms[k]
-                else:
-                    acc_l[p, k, spot : spot + CHUNK] += terms[k]
-
+                acc_r[q + right_layer, k] += total[k]
     def reduced(a, c, layer):
         slot = (a * 6 + c) * 3 + layer
         terms = [jnp.sum(acc_r[slot, k], 0, keepdims=True) for k in range(4)]
@@ -266,10 +269,10 @@
         halo_d.start()
 
         def first_part(index):
-            for c in (0, 1):
-                prepare_own(e, index // 2, index % 2 * 2 + c)
-
-        loop(8, first_part)
+            for c in range(4):
+                prepare_own(e, index, c)
+
+        loop(4, first_part)
 
         def clear(index):
             for number in range(18):
@@ -294,18 +297,19 @@
         loop(16, prepare_above)
 
         def column_part(index):
-            a = index // 2
+            a = index
 
             def where_is(c):
                 return a * 4 + c, (a * 6 + c + 1) * 3, (13 - di) * 32 - (1 - 2 * di) * 32 + (a * 4 + c) * 2
 
-            for c in (index % 2, index % 2 + 2):
+            for c in range(4):
                 p, q, core = where_is(c)
                 tiles(p, q, CENTRE, core, ((0, (0, 1), (1,)), (1, (1,), ())), True, ((0, 0), (1, 1)))
-            p, q, core = where_is(index % 2 + 2 * di)
-            tiles(p, q, CENTRE, core, ((2, (0,), (0,)),))
-
-        loop(8, column_part)
+            for c in range(2):
+                p, q, core = where_is(c + 2 * di)
+                tiles(p, q, CENTRE, core, ((2, (0,), (0,)),))
+
+        loop(4, column_part)
 
         def pick(values, default, at):
             for limit, value in reversed(values):
@@ -324,17 +328,20 @@
             core = (base + 1 - base // 13) * 32 + (a * 4 + c) * 2
             return a * 4 + c, ((a + oa) * 6 + c + 1 + oc) * 3, (oa + 1) * 3 + oc + 1, core
 
-        def lead(place):
+        def lead(place, buffer):
             p, q, entry, core = place
             for layer, rows in ((0, 2 * W), (1, 2 * W), (2, W)):
-                ready[layer * 2 * W : layer * 2 * W + rows] = jnp.dot(
+                ready[buffer, layer * 2 * W : layer * 2 * W + rows] = jnp.dot(
                     lefts[p, 0:rows], right_side(entry, q + layer), preferred_element_type=F32
                 )
 
-        def pair_part(it, carry):
-            place, following = carry
-            tiles(*place, ((0, (0, 1), (0, 1)), (1, (0, 1), (0, 1)), (2, (0,), (0,))), follow=lambda: lead(following))
-            return following, locate(lax.rem(it + 2, 64))
+        def pair_part(number, carry):
+            work = ((0, (0, 1), (0, 1)), (1, (0, 1), (0, 1)), (2, (0,), (0,)))
+            for buffer in (0, 1):
+                tiles(*carry[buffer], work, buffer=buffer)
+            for buffer in (0, 1):
+                lead(carry[2 + buffer], buffer)
+            return carry[2], carry[3], locate(lax.rem(2 * number + 4, 64)), locate(lax.rem(2 * number + 5, 64))
 
         def phase_part(phase, carry):
 
@@ -385,12 +392,13 @@
                 back_cm.start()
 
             start, stop = (pick(((1, x), (2, y), (3, z), (4, w)), v, phase) for x, y, z, w, v in zip(
-                (0, 11), (11, 23), (23, 46), (46, 55), (55, 64)))
+                (0, 5), (5, 11), (11, 23), (23, 27), (27, 32)))
             return lax.fori_loop(start, stop, pair_part, carry)
 
-        begin = locate(jnp.int32(0))
-        lead(begin)
-        lax.fori_loop(0, 5, phase_part, (begin, locate(jnp.int32(1))))
+        begin = tuple(locate(jnp.int32(number)) for number in range(4))
+        lead(begin[0], 0)
+        lead(begin[1], 1)
+        lax.fori_loop(0, 5, phase_part, begin)
 
         back_cp.wait_recv()
         back_cm.wait_recv()
@@ -408,8 +416,8 @@
         back_d.start()
 
         def collect(number):
-            for index in (number * 2, number * 2 + 1):
-                a, c = index // 4, index % 4
+            for a, c in ((number, c) for c in range(4)):
+                index = a * 4 + c
                 halves = [[], []]
                 for layer in (0, 1):
                     sums = [acc_l[index, k, layer * W : layer * W + W] for k in range(4)]
@@ -428,7 +436,7 @@
                 for layer in (0, 1):
                     own[a, c, layer] = left[0:8, layer * W : layer * W + W] + reduced(a, c + 1, layer)
 
-        loop(8, collect)
+        loop(4, collect)
         for c in range(4):
             for layer in (0, 1):
                 own[0, c, layer] += in_a[e, c + 1, layer]
@@ -498,7 +506,7 @@
             pltpu.VMEM((9, 8, W), F32),
             pltpu.VMEM((W, 6 * W), BF16),
             pltpu.VMEM((2, 16, 2 * W), BF16),
-            pltpu.VMEM((5 * W, 2 * W), F32),
+            pltpu.VMEM((2, 5 * W, 2 * W), F32),
             pltpu.VMEM((2, 5, 6, 3, 8, W), F32),
             pltpu.VMEM((90, 32, 2 * W), BF16),
             pltpu.VMEM((90, 32, W), BF16),

time: 108 us -> 99 us (0.917)
  Pallas kernels: 104 us -> 95.2 us
    pallas_call x1, Pallas kernels: 104 us -> 95.2 us  [shards(): pl.pallas_call(body, out_shape=(jax.ShapeDtypeStruct((4, 4, 4, 2, W), F32...]
where the time goes in v3:
time: 99 us; the launch traced here: 98.8 us
  Pallas kernels  95.2 us (96%)
  local copies, waits for them, and re-layouts  3.01 us (3%)
    pallas_call x1, Pallas kernels, shards(): pl.pallas_call(body, out_shape=(jax.ShapeDtypeStruct((4, 4, 4, 2, W), F32...  95.2 us
    unnamed x11, local copies, waits for them, and re-layouts  2.81 us

profile of v3, /device:TPU:1, one launch (start us, length us, event | category | flops | bytes accessed | tf_op | source)
XLA Modules:
  0.0 98.8 jit_solution(17256510855344833635)
XLA Ops:
  0.6 0.9 copy.7
  1.6 0.0 copy-start
  1.6 0.0 copy-start.1
  1.6 0.0 copy-start.2
  1.6 0.0 copy-start.3
  1.6 0.2 reshape.7.refs_4_
  1.8 0.6 copy-done
  2.4 0.0 copy-done.1
  2.4 0.0 copy-done.2
  2.4 0.0 copy-done.3
  2.4 95.2 %sph_step.1 = (f32[4,4,4,2,128]{4,3,2,1,0:T(2,128)S(1)}, f32[7,4,4,2,128]{4,3,2,1,0:T(2,128)S(1)}) custom-call(f32[3,4,4,2,128]{4,3,2,1,0:T(2,128)S(1)} %copy-done, f32[3,4,4,2,128]{4,3,2,1,0:T(2,128)S(1)} %copy-done.1, f32[4,4,2,128]{3,2,1,0:T(2,128)S(1)} %copy-done.2, f32[4,4,2,128]{3,2,1,0:T(2,128)S(1)} %copy-done.3, s32[832]{0:T(1024)S(1)} %reshape.7.refs_4_), custom_call_target="tpu_custom_call" | custom-call | tf_op jit(solution)/shard_map/sph_step/pallas_call | solution.py:496
  97.6 0.6 copy.10
  98.2 0.6 copy.11
Async XLA Ops:
  1.6 0.8 copy-start
  1.6 0.8 copy-start.1
  1.6 0.8 copy-start.2
  1.6 0.8 copy-start.3

commit v4 on v3

--- a/solution.py
+++ b/solution.py
@@ -116,7 +116,6 @@
     barrier = pltpu.get_barrier_semaphore()
     for device in (prev_a, next_a, prev_c, next_c, other):
         pl.semaphore_signal(barrier, inc=1, device_id=device, device_id_type=MESH)
-    pl.semaphore_wait(barrier, 5)
 
     def depth_of(layer):
         return (1 - di) + layer * (2 * di - 1)
@@ -164,9 +163,6 @@
             f0, f1, f2 = split3(flat)
             stack = jnp.concatenate([d0, d0, d1, d1, d0, d2, one, one, one, d0, d1, d2, one, f0, f1, f2], 0)
             lefts[a * 4 + c, layer * W : layer * W + W] = stack.T.astype(BF16)
-        wide = jnp.dot(lefts[a * 4 + c], spread[...], preferred_element_type=F32)
-        for k in range(6):
-            cols[a * 4 + c, k] = wide[:, k * W : k * W + W]
 
     def right_side(entry, slot):
         solid = fixed[slot]
@@ -239,9 +235,8 @@
             return carry
         lax.fori_loop(0, count, run, 0)
 
-    def fill(index):
-        a, c = index // 4, index % 4
-        for layer in (0, 1):
+    def fill(a):
+        for c, layer in ((c, layer) for c in range(4) for layer in (0, 1)):
             at = pl.ds(depth_of(layer), 1)
             lines = [off[k, a, c, at, :] - 0.5 for k in range(3)] + [vel[k, a, c, at, :] for k in range(3)]
             lines += [den[a, c, at, :], mas[a, c, at, :]]
@@ -262,7 +257,8 @@
     upper = lax.broadcasted_iota(jnp.int32, (16, 2 * W), 1) % W // 64
     picks[0] = jnp.where(pick_row == 3 + upper, -1.0, 0.0).astype(BF16)
     picks[1] = jnp.where(pick_row == 5 + upper, jnp.where(upper == 0, -1.0, 1.0), 0.0).astype(BF16)
-    loop(16, fill)
+    loop(4, fill)
+    pl.semaphore_wait(barrier, 5)
 
     def evaluate(e):
         halo_d, halo_cm, halo_cp, halo_a, back_a, back_cp, back_cm, back_d = copies(e)
@@ -271,6 +267,12 @@
         def first_part(index):
             for c in range(4):
                 prepare_own(e, index, c)
+            for c in (0, 2):
+                both = lefts[pl.ds(index * 4 + c, 2)].reshape(4 * W, W)
+                wide = jnp.dot(both, spread[...], preferred_element_type=F32)
+                for k in range(6):
+                    for half in (0, 1):
+                        cols[index * 4 + c + half, k] = wide[half * 2 * W : half * 2 * W + 2 * W, k * W : k * W + W]
 
         loop(4, first_part)
 
@@ -283,18 +285,19 @@
 
         halo_d.wait_recv()
 
-        def flip(index):
-            a, c = index // 4, index % 4
-            raw[e, a, c + 1, 2] = raw[e, a, c + 1, 2] * mirror
-
-        loop(16, flip)
+        def flip(a):
+            for c in range(4):
+                raw[e, a, c + 1, 2] = raw[e, a, c + 1, 2] * mirror
+
+        loop(4, flip)
         halo_cm.start()
         halo_cp.start()
 
-        def prepare_above(index):
-            prepare_right(e, index // 4, index % 4 + 1, 2)
-
-        loop(16, prepare_above)
+        def prepare_above(a):
+            for c in range(4):
+                prepare_right(e, a, c + 1, 2)
+
+        loop(4, prepare_above)
 
         def column_part(index):
             a = index
@@ -403,11 +406,11 @@
         back_cp.wait_recv()
         back_cm.wait_recv()
 
-        def give_above(index):
-            a, c = index // 4, index % 4
-            net[e, a, c + 1, 2] = reduced(a, c + 1, 2)
-
-        loop(16, give_above)
+        def give_above(a):
+            for c in range(4):
+                net[e, a, c + 1, 2] = reduced(a, c + 1, 2)
+
+        loop(4, give_above)
         for c in range(4):
             net[e, 0, c + 1, 2] += in_a[e, c + 1, 2]
         for a in range(4):
@@ -447,29 +450,35 @@
             own[0, 3, layer] += in_cm[e, layer]
         back_d.wait_recv()
 
-        def finish(index):
-            a, c = index // 4, index % 4
-            for layer in (0, 1):
-                state = raw[0, a, c + 1, layer]
-                total = own[a, c, layer]
-                if layer == 0:
-                    total = total + in_d[e, a, c] * mirror
-                rate = total * (-KERNEL / state[7:8]) + gravity
-                speed = state + HALF * rate
+        def settled(a, c, layer):
+            state = raw[0, a, c + 1, layer]
+            total = own[a, c, layer]
+            if layer == 0:
+                total = total + in_d[e, a, c] * mirror
+            return state, total * (-KERNEL / state[7:8]) + gravity
+
+        @pl.when(e == 0)
+        def _():
+            def half_way(a):
                 keep = (row_id >= 3) & (row_id < 7)
-
-                @pl.when(e == 0)
-                def _():
-                    moved_place = state + HALF * pltpu.roll(state, 5, 0)
-                    raw[1, a, c + 1, layer] = jnp.where(keep, speed, jnp.where(row_id < 3, moved_place, state))
-
-                @pl.when(e == 1)
-                def _():
+                for c, layer in ((c, layer) for c in range(4) for layer in (0, 1)):
+                    state, rate = settled(a, c, layer)
+                    place = state + HALF * pltpu.roll(state, 5, 0)
+                    raw[1, a, c + 1, layer] = jnp.where(
+                        keep, state + HALF * rate, jnp.where(row_id < 3, place, state))
+
+            loop(4, half_way)
+
+        @pl.when(e == 1)
+        def _():
+            def finish(a):
+                for c, layer in ((c, layer) for c in range(4) for layer in (0, 1)):
+                    state, rate = settled(a, c, layer)
                     at = pl.ds(depth_of(layer), 1)
-                    start = jnp.where(row_id == 2, state * sign, state)
+                    turn = jnp.where((row_id == 2) | (row_id == 5), sign, 1.0)
+                    start = state * turn
                     start = jnp.where(row_id < 3, start + 0.5, start)
-                    start = jnp.where(row_id == 5, start * sign, start)
-                    rate_g = jnp.where(row_id == 5, rate * sign, rate)
+                    rate_g = rate * turn
                     corr = start + HALF * rate_g
                     place = start + HALF * pltpu.roll(corr, 5, 0)
                     new = jnp.where(row_id < 3, 2.0 * place - start, 2.0 * corr - start)
@@ -479,7 +488,8 @@
                     for k in range(3):
                         rates[k + 1, a, c, at, :] = rate_g[3 + k : 4 + k]
 
-        loop(16, finish)
+            loop(4, finish)
+
         for item in (halo_d, halo_cm, halo_cp, halo_a, back_a, back_cp, back_cm, back_d):
             item.wait_send()
 

time: 99 us -> 95.8 us (0.968)
  Pallas kernels: 95.2 us -> 91.9 us
    pallas_call x1, Pallas kernels: 95.2 us -> 91.9 us  [shards(): pl.pallas_call(body, out_shape=(jax.ShapeDtypeStruct((4, 4, 4, 2, W), F32...]
where the time goes in v4:
time: 95.8 us; the launch traced here: 95.6 us
  Pallas kernels  91.9 us (96%)
  local copies, waits for them, and re-layouts  3.01 us (3%)
    pallas_call x1, Pallas kernels, shards(): pl.pallas_call(body, out_shape=(jax.ShapeDtypeStruct((4, 4, 4, 2, W), F32...  91.9 us
    unnamed x11, local copies, waits for them, and re-layouts  2.81 us

profile of v4, /device:TPU:1, one launch (start us, length us, event | category | flops | bytes accessed | tf_op | source)
XLA Modules:
  0.0 95.6 jit_solution(2502114046969983783)
XLA Ops:
  0.6 0.9 copy.7
  1.6 0.0 copy-start
  1.6 0.0 copy-start.1
  1.6 0.0 copy-start.2
  1.6 0.0 copy-start.3
  1.6 0.2 reshape.7.refs_4_
  1.8 0.6 copy-done
  2.4 0.0 copy-done.1
  2.4 0.0 copy-done.2
  2.4 0.0 copy-done.3
  2.4 91.9 %sph_step.1 = (f32[4,4,4,2,128]{4,3,2,1,0:T(2,128)S(1)}, f32[7,4,4,2,128]{4,3,2,1,0:T(2,128)S(1)}) custom-call(f32[3,4,4,2,128]{4,3,2,1,0:T(2,128)S(1)} %copy-done, f32[3,4,4,2,128]{4,3,2,1,0:T(2,128)S(1)} %copy-done.1, f32[4,4,2,128]{3,2,1,0:T(2,128)S(1)} %copy-done.2, f32[4,4,2,128]{3,2,1,0:T(2,128)S(1)} %copy-done.3, s32[832]{0:T(1024)S(1)} %reshape.7.refs_4_), custom_call_target="tpu_custom_call" | custom-call | tf_op jit(solution)/shard_map/sph_step/pallas_call | solution.py:506
  94.3 0.6 copy.10
  95.0 0.6 copy.11
Async XLA Ops:
  1.6 0.8 copy-start
  1.6 0.8 copy-start.1
  1.6 0.8 copy-start.2
  1.6 0.8 copy-start.3

commit v5 on v4

--- a/solution.py
+++ b/solution.py
@@ -161,8 +161,12 @@
             parts, flat = prepare_right(e, a, c + 1, layer)
             d0, d1, d2 = parts
             f0, f1, f2 = split3(flat)
-            stack = jnp.concatenate([d0, d0, d1, d1, d0, d2, one, one, one, d0, d1, d2, one, f0, f1, f2], 0)
-            lefts[a * 4 + c, layer * W : layer * W + W] = stack.T.astype(BF16)
+            tail = jnp.concatenate([one[0:1], flat[4:6], jnp.zeros((5, W), F32)], 0)
+            stack = jnp.concatenate([d0, d0, d1, d1, d0, d2, one, one, one, d0, d1, d2, tail, f0, f1, f2], 0)
+            turned = stack.T
+            lefts[a * 4 + c, layer * W : layer * W + W] = turned.astype(BF16)
+            for k in (4, 5):
+                cols[a * 4 + c, k, layer * W : layer * W + W] = jnp.broadcast_to(turned[:, 93 + k : 94 + k], (W, W))
 
     def right_side(entry, slot):
         solid = fixed[slot]
@@ -251,7 +255,7 @@
 
     loop(9, fill_table)
     feature = lax.broadcasted_iota(jnp.int32, (W, W), 0)
-    for k in range(6):
+    for k in range(4):
         spread[:, k * W : k * W + W] = jnp.where((feature >= 104) & (feature % 8 == k), 1.0, 0.0).astype(BF16)
     pick_row = lax.broadcasted_iota(jnp.int32, (16, 2 * W), 0)
     upper = lax.broadcasted_iota(jnp.int32, (16, 2 * W), 1) % W // 64
@@ -270,7 +274,7 @@
             for c in (0, 2):
                 both = lefts[pl.ds(index * 4 + c, 2)].reshape(4 * W, W)
                 wide = jnp.dot(both, spread[...], preferred_element_type=F32)
-                for k in range(6):
+                for k in range(4):
                     for half in (0, 1):
                         cols[index * 4 + c + half, k] = wide[half * 2 * W : half * 2 * W + 2 * W, k * W : k * W + W]
 
@@ -514,7 +518,7 @@
         scratch_shapes=[
             pltpu.VMEM((9, 80, 2 * W), BF16),
             pltpu.VMEM((9, 8, W), F32),
-            pltpu.VMEM((W, 6 * W), BF16),
+            pltpu.VMEM((W, 4 * W), BF16),
             pltpu.VMEM((2, 16, 2 * W), BF16),
             pltpu.VMEM((2, 5 * W, 2 * W), F32),
             pltpu.VMEM((2, 5, 6, 3, 8, W), F32),

time: 95.8 us -> 95.1 us (level)
  no operation moved by 1% of the time
where the time goes in v5:
time: 95.1 us; the launch traced here: 95 us
  Pallas kernels  91.3 us (96%)
  local copies, waits for them, and re-layouts  3.01 us (3%)
    pallas_call x1, Pallas kernels, shards(): pl.pallas_call(body, out_shape=(jax.ShapeDtypeStruct((4, 4, 4, 2, W), F32...  91.3 us
    unnamed x11, local copies, waits for them, and re-layouts  2.81 us

profile of v5, /device:TPU:1, one launch (start us, length us, event | category | flops | bytes accessed | tf_op | source)
XLA Modules:
  0.0 95.0 jit_solution(5835532289584005263)
XLA Ops:
  0.6 0.9 copy.7
  1.6 0.0 copy-start
  1.6 0.0 copy-start.1
  1.6 0.0 copy-start.2
  1.6 0.0 copy-start.3
  1.6 0.2 reshape.7.refs_4_
  1.8 0.6 copy-done
  2.4 0.0 copy-done.1
  2.4 0.0 copy-done.2
  2.4 0.0 copy-done.3
  2.4 91.3 %sph_step.1 = (f32[4,4,4,2,128]{4,3,2,1,0:T(2,128)S(1)}, f32[7,4,4,2,128]{4,3,2,1,0:T(2,128)S(1)}) custom-call(f32[3,4,4,2,128]{4,3,2,1,0:T(2,128)S(1)} %copy-done, f32[3,4,4,2,128]{4,3,2,1,0:T(2,128)S(1)} %copy-done.1, f32[4,4,2,128]{3,2,1,0:T(2,128)S(1)} %copy-done.2, f32[4,4,2,128]{3,2,1,0:T(2,128)S(1)} %copy-done.3, s32[832]{0:T(1024)S(1)} %reshape.7.refs_4_), custom_call_target="tpu_custom_call" | custom-call | tf_op jit(solution)/shard_map/sph_step/pallas_call | solution.py:510
  93.7 0.6 copy.10
  94.3 0.6 copy.11
Async XLA Ops:
  1.6 0.8 copy-start
  1.6 0.8 copy-start.1
  1.6 0.8 copy-start.2
  1.6 0.8 copy-start.3
